TPU v7x, 128 devices: a whole 4x4x4 slice. The times are simulated.
128 devices in a mesh: ctx: 32 (over y, z, x_lo), tp: 4 (over x_hi, core).
Axes of the slice: x: 4 (x_hi: 2, x_lo: 2; x = x_hi * 2 + x_lo), y: 4, z: 4, core: 2. Of those that a mesh axis runs over, the one named last changes fastest.
Arguments:
- residual: bfloat16 [8192, 5120], P('ctx'), may hold values from -24 to 24
- out_grad: bfloat16 [8192, 5120], P('ctx'), may hold values from -6 to 6
- queries: bfloat16 [8192, 2560], P('ctx', 'tp'), may hold values from -6 to 6
- key_rows: bfloat16 [8192, 512], P('ctx', 'tp'), may hold values from -6 to 6
- value_rows: bfloat16 [8192, 512], P('ctx', 'tp'), may hold values from -6 to 6
- doc_ids: int32 [8192], P('ctx'), may hold values from 0 to 7, never falling along the last dimension, each value on 1 to 6144 neighbouring positions
- expert_ids: int32 [8192], P('ctx'), may hold values from 0 to 127, as said below
- norm_gain: bfloat16 [5120], replicated, may hold values from 0.099609375 to 1.8984375
- router_columns: bfloat16 [5120, 4], P(None, 'tp'), may hold values from -0.078125 to 0.078125
- gate_weight: bfloat16 [4, 5120, 8192], P('tp', None, 'ctx'), may hold values from -0.15625 to 0.15625
- up_weight: bfloat16 [4, 5120, 8192], P('tp', None, 'ctx'), may hold values from -0.15625 to 0.15625
- down_weight: bfloat16 [4, 8192, 5120], P('tp', 'ctx'), may hold values from -0.09375 to 0.09375
- out_weight: bfloat16 [2560, 5120], P('tp', 'ctx'), may hold values from -0.125 to 0.125
Outputs:
- residual_grad: bfloat16 [8192, 5120], P('ctx')
- query_grad: bfloat16 [8192, 2560], P('ctx', 'tp')
- key_grad: bfloat16 [8192, 512], P('ctx', 'tp')
- value_grad: bfloat16 [8192, 512], P('ctx', 'tp')
- grad_gate: bfloat16 [4, 5120, 8192], P('tp', None, 'ctx')
- grad_up: bfloat16 [4, 5120, 8192], P('tp', None, 'ctx')
- grad_down: bfloat16 [4, 8192, 5120], P('tp', 'ctx')
Inputs may be any that keep to these rules, and one draw needn't show every extreme that they name: `expert_ids`: in each aligned block of 256 tokens at most 4 tokens name any one expert below 4, and some expert below 4 is named exactly 4 times in every block. `doc_ids`: document numbers never fall along the sequence.
All inputs are finite; a program needn't handle non-finite values.
Results may differ from a plain program's by a relative error of at most 0.03.
Values may be sent and summed in bfloat16 or wider, within the bound.
A program may use at most 128 MiB of HBM per device.

v0:
```python
import jax
import jax.numpy as jnp
from jax import lax
from jax.sharding import PartitionSpec as P

HD = 128
CAPL = 4


EPS = 1e-05
NEG = -1e30


def contract(left, right, left_dim, right_dim):
    return lax.dot_general(
        left, right, (((left_dim,), (right_dim,)), ((), ())), preferred_element_type=jnp.float32
    )


def block_width():
    return 512


def sweep_keys(visits, limits, carry, piece, start):
    key_all, value_all, doc_all = piece
    count = key_all.shape[0]
    width = block_width()

    def advance(index, states):
        first = start + index * width
        key_block = lax.dynamic_slice_in_dim(key_all, index * width, width, 0)
        value_block = lax.dynamic_slice_in_dim(value_all, index * width, width, 0)
        doc_block = lax.dynamic_slice_in_dim(doc_all, index * width, width, 0)
        updated = []
        for visit, limit, state in zip(visits, limits, states):
            last_query, lowest_doc = limit
            needed = (first <= last_query) & (doc_block[width - 1] >= lowest_doc)

            def work(inner, visit=visit):
                return visit(inner, key_block, value_block, doc_block, first)

            updated.append(lax.cond(needed, work, lambda inner: inner, state))
        return tuple(updated)

    return lax.fori_loop(0, count // width, advance, carry)


def head_rows(array, heads):
    length = array.shape[0]
    return array.reshape(length, heads, -1).transpose(1, 0, 2).reshape(heads * length, -1)


def make_group(query_part, grad_part, pos_part, doc_part, heads):
    return (
        head_rows(query_part, heads),
        head_rows(grad_part, heads),
        jnp.tile(pos_part, heads),
        jnp.tile(doc_part, heads),
        jnp.max(pos_part),
        jnp.min(doc_part),
    )


def local(
    residual,
    out_grad,
    queries,
    key_rows,
    value_rows,
    doc_ids,
    expert_ids,
    norm_gain,
    router_columns,
    gate_weight,
    up_weight,
    down_weight,
    out_weight,
):
    ctx_index = lax.axis_index("ctx")
    tp_index = lax.axis_index("tp")
    ctx_count = lax.axis_size("ctx")
    length = residual.shape[0]
    heads = queries.shape[1] // HD
    scale = HD ** (-0.5)
    mine = (expert_ids == tp_index).astype(jnp.int32)
    slot = jnp.cumsum(mine) - mine
    place = ((mine[None, :] > 0) & (slot[None, :] == jnp.arange(CAPL)[:, None])).astype(
        jnp.bfloat16
    )
    rows_hidden = jnp.dot(place, residual, preferred_element_type=jnp.float32).astype(jnp.bfloat16)
    rows_grad = jnp.dot(place, out_grad, preferred_element_type=jnp.float32).astype(jnp.bfloat16)
    key_all, value_all, doc_all, out_full, all_hidden, all_grad = (
        lax.all_gather(key_rows, "ctx", axis=0, tiled=True),
        lax.all_gather(value_rows, "ctx", axis=0, tiled=True),
        lax.all_gather(doc_ids, "ctx", axis=0, tiled=True),
        lax.all_gather(out_weight, "ctx", axis=1, tiled=True),
        lax.all_gather(rows_hidden, "ctx", axis=0, tiled=True),
        lax.all_gather(rows_grad, "ctx", axis=0, tiled=True),
    )
    gain = norm_gain.astype(jnp.float32)
    hidden_all = all_hidden.astype(jnp.float32)
    inverse = lax.rsqrt(jnp.mean(hidden_all * hidden_all, axis=1, keepdims=True) + EPS)
    normed = (hidden_all * inverse * gain).astype(jnp.bfloat16)
    column = router_columns[:, 0]
    score = jax.nn.sigmoid(jnp.dot(normed, column, preferred_element_type=jnp.float32))[:, None]
    routed = (normed.astype(jnp.float32) * score).astype(jnp.bfloat16)
    gate_local = gate_weight[0]
    up_local = up_weight[0]
    down_local = down_weight[0]
    gate = jnp.dot(routed, gate_local, preferred_element_type=jnp.float32)
    upward = jnp.dot(routed, up_local, preferred_element_type=jnp.float32)
    sigma = jax.nn.sigmoid(gate)
    swish = gate * sigma
    active = (swish * upward).astype(jnp.bfloat16)
    active_grad = contract(all_grad, down_local, 1, 1)
    gate_delta = (active_grad * upward * sigma * (1.0 + gate * (1.0 - sigma))).astype(jnp.bfloat16)
    up_delta = (active_grad * swish).astype(jnp.bfloat16)
    grad_down = contract(active, all_grad, 0, 0).astype(jnp.bfloat16)[None]
    grad_gate = contract(routed, gate_delta, 0, 0).astype(jnp.bfloat16)[None]
    grad_up = contract(routed, up_delta, 0, 0).astype(jnp.bfloat16)[None]
    routed_grad = lax.psum_scatter(
        contract(gate_delta, gate_local, 1, 1) + contract(up_delta, up_local, 1, 1),
        "ctx",
        scatter_dimension=0,
        tiled=True,
    )
    first_row = ctx_index * CAPL
    own_normed = lax.dynamic_slice_in_dim(normed, first_row, CAPL, 0).astype(jnp.float32)
    own_score = lax.dynamic_slice_in_dim(score, first_row, CAPL, 0)
    own_hidden = lax.dynamic_slice_in_dim(hidden_all, first_row, CAPL, 0)
    own_inverse = lax.dynamic_slice_in_dim(inverse, first_row, CAPL, 0)
    score_grad = (
        jnp.sum(routed_grad * own_normed, axis=1, keepdims=True) * own_score * (1.0 - own_score)
    )
    normed_grad = routed_grad * own_score + score_grad * column.astype(jnp.float32)[None, :]
    scaled = gain * normed_grad
    rows_out = own_inverse * scaled - own_hidden * own_inverse**3 * jnp.mean(
        scaled * own_hidden, axis=1, keepdims=True
    )
    token_part = jnp.dot(place.T.astype(jnp.float32), rows_out, precision=lax.Precision.HIGHEST)
    moe_grad = lax.psum(token_part, "tp")
    residual_grad = (out_grad.astype(jnp.float32) + moe_grad).astype(jnp.bfloat16)
    attn_sum = contract(residual_grad, out_full, 1, 1)
    attn_grad = attn_sum.astype(jnp.bfloat16)
    groups = [
        make_group(queries, attn_grad, ctx_index * length + jnp.arange(length), doc_ids, heads)
    ]
    limits = [(group[4], group[5]) for group in groups]

    def forward_step(group):
        query_block, grad_block, query_pos, query_doc = (group[0], group[1], group[2], group[3])

        def visit(state, key_block, value_block, doc_block, first):
            top, total, weighted = state
            key_pos = first + jnp.arange(key_block.shape[0])
            logits = contract(query_block, key_block, 1, 1) * scale
            allowed = (key_pos[None, :] <= query_pos[:, None]) & (
                doc_block[None, :] == query_doc[:, None]
            )
            new_top = jnp.maximum(top, jnp.max(jnp.where(allowed, logits, NEG), axis=1))
            factor = jnp.exp(top - new_top)
            weights = jnp.where(allowed, jnp.exp(logits - new_top[:, None]), 0.0)
            prob_grad = contract(grad_block, value_block, 1, 1)
            return (
                new_top,
                total * factor + jnp.sum(weights, axis=1),
                weighted * factor + jnp.sum(weights * prob_grad, axis=1),
            )

        return visit

    forward_visits = [forward_step(group) for group in groups]
    start_state = tuple(
        (
            (
                jnp.full((group[0].shape[0],), NEG, jnp.float32),
                jnp.zeros((group[0].shape[0],), jnp.float32),
                jnp.zeros((group[0].shape[0],), jnp.float32),
            )
            for group in groups
        )
    )
    forward_states = sweep_keys(
        forward_visits, limits, start_state, (key_all, value_all, doc_all), 0
    )

    def backward_step(group, statistics):
        query_block, grad_block, query_pos, query_doc = (group[0], group[1], group[2], group[3])
        top, total, weighted = statistics
        log_total = top + jnp.log(total)
        delta = weighted / total

        def visit(state, key_block, value_block, doc_block, first):
            query_acc, key_acc, value_acc = state
            width = key_block.shape[0]
            key_pos = first + jnp.arange(width)
            logits = contract(query_block, key_block, 1, 1) * scale
            allowed = (key_pos[None, :] <= query_pos[:, None]) & (
                doc_block[None, :] == query_doc[:, None]
            )
            prob = jnp.where(allowed, jnp.exp(logits - log_total[:, None]), 0.0)
            prob_grad = contract(grad_block, value_block, 1, 1)
            logit_grad = (prob * (prob_grad - delta[:, None])).astype(jnp.bfloat16)
            prob_half = prob.astype(jnp.bfloat16)
            query_acc = query_acc + contract(logit_grad, key_block, 1, 0) * scale
            key_part = contract(logit_grad, query_block, 0, 0) * scale
            value_part = contract(prob_half, grad_block, 0, 0)
            key_acc = lax.dynamic_update_slice_in_dim(
                key_acc, lax.dynamic_slice_in_dim(key_acc, first, width, 0) + key_part, first, 0
            )
            value_acc = lax.dynamic_update_slice_in_dim(
                value_acc,
                lax.dynamic_slice_in_dim(value_acc, first, width, 0) + value_part,
                first,
                0,
            )
            return (query_acc, key_acc, value_acc)

        return visit

    backward_visits = [backward_step(group, stats) for group, stats in zip(groups, forward_states)]
    full_length = length * ctx_count
    head_width = key_rows.shape[1]
    back_state = tuple(
        (
            (
                jnp.zeros((group[0].shape[0], HD), jnp.float32),
                jnp.zeros((full_length, head_width), jnp.float32),
                jnp.zeros((full_length, head_width), jnp.float32),
            )
            for group in groups
        )
    )
    back_states = sweep_keys(backward_visits, limits, back_state, (key_all, value_all, doc_all), 0)
    key_acc = back_states[0][1]
    value_acc = back_states[0][2]
    key_sum, value_sum = (
        lax.psum_scatter(key_acc, "ctx", scatter_dimension=0, tiled=True),
        lax.psum_scatter(value_acc, "ctx", scatter_dimension=0, tiled=True),
    )
    query_acc = back_states[0][0]
    count = query_acc.shape[0] // heads
    query_grad = (
        query_acc.reshape(heads, count, HD)
        .transpose(1, 0, 2)
        .reshape(count, heads * HD)
        .astype(jnp.bfloat16)
    )
    return (
        residual_grad,
        query_grad,
        key_sum.astype(jnp.bfloat16),
        value_sum.astype(jnp.bfloat16),
        grad_gate,
        grad_up,
        grad_down,
    )


def solution(mesh):
    in_specs = (
        P("ctx", None),
        P("ctx", None),
        P("ctx", "tp"),
        P("ctx", "tp"),
        P("ctx", "tp"),
        P("ctx"),
        P("ctx"),
        P(),
        P(None, "tp"),
        P("tp", None, "ctx"),
        P("tp", None, "ctx"),
        P("tp", "ctx", None),
        P("tp", "ctx"),
    )
    out_specs = (
        P("ctx", None),
        P("ctx", "tp"),
        P("ctx", "tp"),
        P("ctx", "tp"),
        P("tp", None, "ctx"),
        P("tp", None, "ctx"),
        P("tp", "ctx", None),
    )
    return jax.shard_map(local, mesh=mesh, in_specs=in_specs, out_specs=out_specs, check_vma=False)
```

profile of v0, /device:TPU:0, one launch (start us, length us, event | category | flops | bytes accessed | tf_op | source)
XLA Modules:
  0.0 1913.6 jit_solution(917085973643296459)
XLA Ops:
  7.2 0.8 fusion.71
  8.6 0.8 bitcast_subtract_fusion
  9.4 2.8 fusion.43
  12.3 2.8 fusion.44
  15.2 152.2 %all-gather.15.cloned.1.call-done = bf16[32,4,5120]{2,1,0:T(4,128)(2,1)} async-done(((bf16[1,4,5120]{2,1,0:T(4,128)(2,1)}), bf16[32,4,5120]{2,1,0:T(4,128)(2,1)}) %all-gather.15.cloned.1.call-update) | async-done | bytes 1310736 | tf_op jit(solution)/shard_map/all_gather | solution.py:97
  167.3 3.3 reshape.121
  170.6 2.2 multiply_reduce_fusion
  174.0 1.3 copy-done.9
  176.5 145.7 %all-gather.17.cloned.1.call-done = bf16[32,4,5120]{2,1,0:T(4,128)(2,1)} async-done(((bf16[1,4,5120]{2,1,0:T(4,128)(2,1)}), bf16[32,4,5120]{2,1,0:T(4,128)(2,1)}) %all-gather.17.cloned.1.call-update) | async-done | bytes 1310736 | tf_op jit(solution)/shard_map/all_gather | solution.py:98
  322.3 3.3 reshape.118
  325.6 3.1 multiply_convert_fusion.3
  328.7 1.0 fusion.45
  329.7 0.7 copy-done.10
  330.5 2.5 convolution_add_fusion
  334.9 320.1 %all-reduce.6.cloned.1.call-done = f32[128,5120]{1,0:T(8,128)} async-done(((f32[128,5120]{1,0:T(8,128)}), f32[128,5120]{1,0:T(8,128)}) %all-reduce.6.cloned.1.call-update) | async-done | bytes 2621456
  655.1 1.1 multiply_reduce_fusion.2
  656.3 1.2 multiply_reduce_fusion.1
  657.5 5.6 fusion.59
  666.1 82.7 %all-gather.2 = s32[32,1,256]{2,1,0:T(1,128)S(1)} all-gather(s32[1,1,256]{2,1,0:T(1,128)S(1)} %bitcast.108), channel_id=1, replica_groups=mesh['ctx'=32,'tp'=4] {'ctx'}, dimensions={0}, use_global_device_ids=true | all-gather | bytes 33792 | tf_op jit(solution)/shard_map/all_gather | solution.py:95
  749.5 24.4 %all-reduce.4.cloned.1.call-done = f32[256,5120]{1,0:T(8,128)} async-done(((f32[256,5120]{1,0:T(8,128)}), f32[256,5120]{1,0:T(8,128)}) %all-reduce.4.cloned.1.call-update) | async-done | bytes 5242896 | tf_op jit(solution)/shard_map/psum | solution.py:141
  773.9 5.5 add_convert_fusion
  779.4 170.0 %all-gather.13.cloned.1.call-done = bf16[640,5120]{0,1:T(8,128)(2,1)} async-done(((bf16[640,160]{0,1:T(8,128)(2,1)}), bf16[640,5120]{0,1:T(8,128)(2,1)}) %all-gather.13.cloned.1.call-update) | async-done | bytes 6553616 | tf_op jit(solution)/shard_map/all_gather | solution.py:96
  949.3 5.9 convolution_convert_fusion.5
  955.6 149.6 %all-gather.11.cloned.1.call-done = bf16[8192,128]{1,0:T(8,128)(2,1)} async-done(((bf16[256,128]{1,0:T(8,128)(2,1)}), bf16[8192,128]{1,0:T(8,128)(2,1)}) %all-gather.11.cloned.1.call-update) | async-done | bytes 2097168 | tf_op jit(solution)/shard_map/all_gather | solution.py:94
  1105.2 156.9 %all-gather.9.cloned.1.call-done = bf16[8192,128]{1,0:T(8,128)(2,1)} async-done(((bf16[256,128]{1,0:T(8,128)(2,1)}), bf16[8192,128]{1,0:T(8,128)(2,1)}) %all-gather.9.cloned.1.call-update) | async-done | bytes 2097168 | tf_op jit(solution)/shard_map/all_gather | solution.py:93
  1262.1 47.1 %while.36 = (s32[]{:T(128)}, f32[1280]{0:T(1024)S(1)}, f32[1280]{0:T(1024)S(1)}, f32[1280]{0:T(1024)S(1)}, s32[]{:T(128)}, /*index=5*/s32[8192]{0:T(1024)S(1)}, ...) while((s32[]{:T(128)}, f32[1280]{0:T(1024)S(1)}, ...), condition=%wide.region_15.16_spmd.clone, body=%wide.region_9.15_spmd.clone.sunk | while | flops 348000512 | bytes 8957325 | solution.py:45
  1264.7 4.4 conditional.6
  1264.8 1.6 select_reduce_fusion
  1266.5 0.7 fusion.10
  1267.2 1.9 fusion.11
  1309.2 2.2 broadcast.113
  1311.4 2.2 broadcast.113.clone
  1313.7 53.9 %while.37 = (s32[]{:T(128)}, f32[1280,128]{1,0:T(8,128)S(1)}, f32[8192,128]{1,0:T(8,128)}, f32[8192,128]{1,0:T(8,128)}, s32[]{:T(128)}, /*index=5*/s32[8192]{0:T...) while((s32[]{:T(128)}, f32[1280,128]{1,0:T(8,128)S(1)}, ...), condition=%wide.region_19.20_spmd.clone, body=%wide.region_16.0_spmd.clone.sunk | while | flops 845939200 | bytes 26410996 | solution.py:45
  1316.3 11.4 conditional.7
  1316.4 1.8 fusion.19
  1318.2 1.5 copy-done.2
  1319.7 1.4 fusion.22
  1321.1 2.2 fusion.27
  1323.3 3.0 fusion.31
  1326.2 1.5 fusion.23
  1369.2 2.4 fusion.42
  1371.6 2.5 fusion.40
  1374.0 2.5 fusion.41
  1376.7 0.9 copy.37
  1377.6 354.6 %reduce-scatter.3.cloned.1.call-done = f32[256,128]{1,0:T(8,128)} async-done(((f32[8192,128]{1,0:T(8,128)}), f32[256,128]{1,0:T(8,128)}) %reduce-scatter.3.cloned.1.call-update) | async-done | bytes 131088 | tf_op jit(solution)/shard_map/reduce_scatter | solution.py:238
  1732.2 1.5 convert_element_type.124
  1733.7 171.8 %reduce-scatter.5.cloned.1.call-done = f32[256,128]{1,0:T(8,128)} async-done(((f32[8192,128]{1,0:T(8,128)}), f32[256,128]{1,0:T(8,128)}) %reduce-scatter.5.cloned.1.call-update) | async-done | bytes 131088 | tf_op jit(solution)/shard_map/reduce_scatter | solution.py:239
  1905.5 1.5 convert_element_type.125
  (183 shorter events, 32.2 us)
Async XLA Ops:
  7.2 168.8 %copy-start = (bf16[1,5120,256]{2,1,0:T(8,128)(2,1)S(1)}, bf16[1,5120,256]{2,1,0:T(8,128)(2,1)}, u32[]{:S(2)}) copy-start(bf16[1,5120,256]{2,1,0:T(8,128)(2,1)} %param.30) | copy-start | bytes 7864324
  7.2 160.1 %all-gather.15.cloned.1.call-start = ((), (), s32[]{:S(2)}) async-start(), calls=%async_computation.8 | async-start | bytes 1351680 | tf_op jit(solution)/shard_map/all_gather | solution.py:97
  9.4 5.8 copy-start.14
  12.2 310.1 %all-gather.17.cloned.1.call-start = ((), (), s32[]{:S(2)}) async-start(), calls=%async_computation.9 | async-start | bytes 1351680 | tf_op jit(solution)/shard_map/all_gather | solution.py:98
  15.1 640.0 %all-reduce.6.cloned.1.call-start = ((), (), s32[]{:S(2)}) async-start(), calls=%async_computation.10 | async-start | bytes 5242880
  170.6 2.5 copy-start.7
  172.8 0.8 copy-start.13
  173.1 2.2 copy-start.9
  173.6 2.3 copy-start.3
  328.7 1.7 copy-start.10
  332.9 0.7 copy-start.15
  333.0 440.9 %all-reduce.4.cloned.1.call-start = ((), (), s32[]{:S(2)}) async-start(), calls=%async_computation.2 | async-start | bytes 10485760 | tf_op jit(solution)/shard_map/psum | solution.py:141
  663.1 2.0 copy-start.11
  663.1 2.4 copy-start.12
  663.1 286.2 %all-gather.13.cloned.1.call-start = ((), (), s32[]{:S(2)}) async-start(), calls=%async_computation.5 | async-start | bytes 6758400 | tf_op jit(solution)/shard_map/all_gather | solution.py:96
  663.7 441.4 %all-gather.11.cloned.1.call-start = ((), (), s32[]{:S(2)}) async-start(), calls=%async_computation.4 | async-start | bytes 2162688 | tf_op jit(solution)/shard_map/all_gather | solution.py:94
  664.3 597.8 %all-gather.9.cloned.1.call-start = ((), (), s32[]{:S(2)}) async-start(), calls=%async_computation.3 | async-start | bytes 2162688 | tf_op jit(solution)/shard_map/all_gather | solution.py:93
  665.1 1067.1 %reduce-scatter.3.cloned.1.call-start = ((), (), s32[]{:S(2)}) async-start(), calls=%async_computation.6 | async-start | bytes 4325376 | tf_op jit(solution)/shard_map/reduce_scatter | solution.py:238
  1318.2 1.5 copy-start.2
  1367.6 0.9 copy-start.5
  1367.7 1.5 copy-start.8
  1367.7 537.9 %reduce-scatter.5.cloned.1.call-start = ((), (), s32[]{:S(2)}) async-start(), calls=%async_computation.7 | async-start | bytes 4325376 | tf_op jit(solution)/shard_map/reduce_scatter | solution.py:239
  1369.2 2.4 copy-start.4
  1371.6 535.5 %copy-start.1 = (bf16[1,5120,256]{2,1,0:T(8,128)(2,1)S(1)}, bf16[1,5120,256]{2,1,0:T(8,128)(2,1)}, u32[]{:S(2)}) copy-start(bf16[1,5120,256]{2,1,0:T(8,128)(2,1)} %param.30) | copy-start | bytes 7864324
  1374.0 2.5 copy-start.6
Sparse Core Ops, SparseCore 0:
  12.3 154.9 all-gather.14
  169.5 152.6 all-gather.16
  333.1 321.9 all-reduce.5
  663.3 110.5 all-reduce.3
  775.4 173.9 all-gather.12
  950.8 154.2 all-gather.10
  1106.8 155.2 all-gather.8
  1367.8 364.3 reduce-scatter.2
  1734.6 170.9 reduce-scatter.4
where the time goes:
time: 1900 us; the launch traced here: 1910 us
  waiting for transfers between devices  1650 us (87%)
  blocking collectives  82.7 us (4%)
  loops' own time  63.8 us (3%)
  matrix products  45.9 us (2%)
  local copies, waits for them, and re-layouts  40.7 us (2%)
    reduce_scatter x1, waiting for transfers between devices, local(): lax.psum_scatter(key_acc, 'ctx', scatter_dimension=0, tiled=True)  355 us
    unnamed x10, waiting for transfers between devices  323 us
    reduce_scatter x1, waiting for transfers between devices, local(): lax.psum_scatter(value_acc, 'ctx', scatter_dimension=0, tiled=True)  172 us
    all_gather x1, waiting for transfers between devices, local(): lax.all_gather(out_weight, 'ctx', axis=1, tiled=True)  170 us
    all_gather x1, waiting for transfers between devices, local(): lax.all_gather(key_rows, 'ctx', axis=0, tiled=True)  157 us
    all_gather x1, waiting for transfers between devices, local(): lax.all_gather(rows_hidden, 'ctx', axis=0, tiled=True)  152 us
    all_gather x1, waiting for transfers between devices, local(): lax.all_gather(value_rows, 'ctx', axis=0, tiled=True)  150 us
    all_gather x1, waiting for transfers between devices, local(): lax.all_gather(rows_grad, 'ctx', axis=0, tiled=True)  146 us
  transfers between devices with their start and end apart: 9, of which 9 were waited for; matrix products, arithmetic and copies ran while one was open for 2% of the time, Pallas kernels for 0%

commit v1 on v0

v1 whole, which is shorter than its diff:
```python
import functools

import jax
import jax.numpy as jnp
from jax import lax
from jax.experimental import pallas as pl
from jax.experimental.pallas import tpu as pltpu
from jax.sharding import PartitionSpec as P

HD = 128
CAPL = 4
EPS = 1e-05
NEG = -1e30
LOG2E = 1.4426950408889634
MESH = pl.DeviceIdType.MESH
NY, NZ, NX = 4, 4, 2
CTX = NY * NZ * NX
TP = 4


def contract(left, right, left_dim, right_dim):
    return lax.dot_general(
        left, right, (((left_dim,), (right_dim,)), ((), ())), preferred_element_type=jnp.float32
    )


def place_of():
    me = lax.axis_index("ctx")
    return me // (NZ * NX), (me // NX) % NZ, me % NX


def at(y, z, x):
    return {"ctx": y * (NZ * NX) + z * NX + x}


def signal(device):
    pl.semaphore_signal(
        pltpu.get_barrier_semaphore(), inc=1, device_id=device, device_id_type=MESH
    )


def remote(src, dst, send, recv, device):
    return pltpu.make_async_remote_copy(
        src_ref=src, dst_ref=dst, send_sem=send, recv_sem=recv, device_id=device, device_id_type=MESH
    )


class Gather:
    def __init__(self, src, buf, order, send, recv, local):
        self.src, self.buf, self.order = src, buf, order
        self.send, self.recv, self.local = send, recv, local

    def copy(self, src, dst, k, device):
        return remote(src, dst, self.send.at[k], self.recv.at[k], device)

    def along_z(self, step):
        return (self.order == 0) == (step in (2, 3))

    def slab(self, step, offset, half):
        y, z, x = place_of()
        buf = self.buf
        if self.along_z(step):
            z = (z + offset) % NZ
        else:
            y = (y + offset) % NY
        if step in (2, 3):
            return buf.at[y, z] if half is None else buf.at[y, z, half]
        if self.along_z(step):
            return buf.at[:, z] if half is None else buf.at[2 * half : 2 * half + 2, z]
        return buf.at[y] if half is None else buf.at[y, 2 * half : 2 * half + 2]

    def device(self, step, offset):
        y, z, x = place_of()
        if self.along_z(step):
            return at(y, (z + offset) % NZ, x)
        return at((y + offset) % NY, z, x)

    def sends(self, step):
        y, z, x = place_of()
        if step == 1:
            return [self.copy(self.src, self.buf.at[y, z, x], 0, at(y, z, 1 - x))]
        copies = []
        for i, d in enumerate((1, 3)):
            k = 1 + 2 * (step - 2) + i
            part = self.slab(step, 0, None) if step in (2, 4) else self.slab(step, 4 - d, i)
            copies.append(self.copy(part, part, k, self.device(step, d)))
        return copies

    def receives(self, step):
        y, z, x = place_of()
        if step == 1:
            part = self.buf.at[y, z, 1 - x]
            return [self.copy(part, part, 0, at(y, z, 1 - x))]
        copies = []
        for i, d in enumerate((1, 3)):
            k = 1 + 2 * (step - 2) + i
            part = self.slab(step, 4 - d, None) if step in (2, 4) else self.slab(step, 2, i)
            copies.append(self.copy(part, part, k, self.device(step, d)))
        return copies

    def own(self):
        y, z, x = place_of()
        return pltpu.make_async_copy(self.src, self.buf.at[y, z, x], self.local)

    def start(self, step):
        if step == 1:
            self.own().start()
        for copy in self.sends(step):
            copy.start()

    def arrive(self, step):
        if step == 1:
            self.own().wait()
        for copy in self.receives(step):
            copy.wait_recv()

    def finish(self):
        for step in range(1, 6):
            for copy in self.sends(step):
                copy.wait_send()


def gather_kernel(orders, *refs):
    n = len(orders)
    ins, outs, (send, recv, local) = refs[:n], refs[n : 2 * n], refs[2 * n :]
    y, z, x = place_of()
    signal(at(y, z, 1 - x))
    for d in (1, 3):
        signal(at(y, (z + d) % NZ, x))
        signal(at((y + d) % NY, z, x))
    pl.semaphore_wait(pltpu.get_barrier_semaphore(), 5)
    parts = [
        Gather(ins[i], outs[i], orders[i], send.at[i], recv.at[i], local.at[i]) for i in range(n)
    ]
    for part in parts:
        part.start(1)
    for step in range(2, 6):
        for part in parts:
            part.arrive(step - 1)
            part.start(step)
    for part in parts:
        part.arrive(5)
    for part in parts:
        part.finish()


def gather(arrays, orders, collective_id):
    n = len(arrays)
    return pl.pallas_call(
        functools.partial(gather_kernel, orders),
        out_shape=[jax.ShapeDtypeStruct((NY, NZ, NX) + a.shape, a.dtype) for a in arrays],
        in_specs=[pl.BlockSpec(memory_space=pltpu.VMEM)] * n,
        out_specs=[pl.BlockSpec(memory_space=pltpu.VMEM)] * n,
        scratch_shapes=[
            pltpu.SemaphoreType.DMA((n, 9)),
            pltpu.SemaphoreType.DMA((n, 9)),
            pltpu.SemaphoreType.DMA((n,)),
        ],
        compiler_params=pltpu.CompilerParams(
            collective_id=collective_id, has_side_effects=True, vmem_limit_bytes=50 << 20
        ),
    )(*arrays)


def fold_rows(column):
    row = lax.broadcasted_iota(jnp.int32, (16, 16), 0) % CAPL
    col = lax.broadcasted_iota(jnp.int32, (16, 16), 1) % CAPL
    same = (row == col).astype(jnp.float32)
    wide = jnp.broadcast_to(column, (16, 128))
    return jnp.dot(
        same, wide, precision=lax.Precision.HIGHEST, preferred_element_type=jnp.float32
    )[:, :1]


def rows_kernel(
    part, normed, hidden, gain, column, score, inverse, out, slots, send, recv, tsend, trecv, local
):
    me = lax.axis_index("ctx")
    tp = lax.axis_index("tp")

    def greet(d, _):
        signal({"ctx": (me + d) % CTX})
        return 0

    lax.fori_loop(1, CTX, greet, 0)
    for d in range(1, TP):
        signal({"tp": (tp + d) % TP})
    pl.semaphore_wait(pltpu.get_barrier_semaphore(), CTX - 1 + TP - 1)

    def launch(d, _):
        to = (me + d) % CTX
        remote(part.at[to], slots.at[me], send.at[d], recv.at[d], {"ctx": to}).start()
        return 0

    lax.fori_loop(1, CTX, launch, 0)

    def collect(d, total):
        source = (me + CTX - d) % CTX
        remote(part.at[me], slots.at[source], send.at[d], recv.at[d], {"ctx": source}).wait_recv()
        return total + slots[source].astype(jnp.float32)

    routed_grad = lax.fori_loop(1, CTX, collect, part[me].astype(jnp.float32))
    normed_v = normed[...].astype(jnp.float32)
    hidden_v = hidden[...].astype(jnp.float32)
    score_v = score[:, :1]
    inverse_v = inverse[:, :1]
    dots = fold_rows(jnp.sum(routed_grad * normed_v, axis=1, keepdims=True))
    score_grad = dots * score_v * (1.0 - score_v)
    scaled = gain[...] * (routed_grad * score_v + score_grad * column[...])
    mean = fold_rows(jnp.sum(scaled * hidden_v, axis=1, keepdims=True)) * (1.0 / (4 * 1280))
    rows = inverse_v * scaled - hidden_v * (inverse_v * inverse_v * inverse_v) * mean
    out[tp] = rows.astype(jnp.bfloat16)
    for d in range(1, TP):
        remote(
            out.at[tp], out.at[tp], tsend.at[d], trecv.at[d], {"tp": (tp + d) % TP}
        ).start()
    for d in range(1, TP):
        source = (tp + TP - d) % TP
        remote(
            out.at[source], out.at[source], tsend.at[d], trecv.at[d], {"tp": source}
        ).wait_recv()
    for d in range(1, TP):
        remote(
            out.at[tp], out.at[tp], tsend.at[d], trecv.at[d], {"tp": (tp + d) % TP}
        ).wait_send()

    def drain(d, _):
        to = (me + d) % CTX
        remote(part.at[to], slots.at[me], send.at[d], recv.at[d], {"ctx": to}).wait_send()
        return 0

    lax.fori_loop(1, CTX, drain, 0)


def expert_rows(part, normed, hidden, gain, column, score, inverse, collective_id):
    return pl.pallas_call(
        rows_kernel,
        out_shape=jax.ShapeDtypeStruct((TP, 16, 1280), jnp.bfloat16),
        in_specs=[pl.BlockSpec(memory_space=pltpu.VMEM)] * 7,
        out_specs=pl.BlockSpec(memory_space=pltpu.VMEM),
        scratch_shapes=[
            pltpu.VMEM((CTX, 16, 1280), jnp.bfloat16),
            pltpu.SemaphoreType.DMA((CTX,)),
            pltpu.SemaphoreType.DMA((CTX,)),
            pltpu.SemaphoreType.DMA((TP,)),
            pltpu.SemaphoreType.DMA((TP,)),
            pltpu.SemaphoreType.DMA,
        ],
        compiler_params=pltpu.CompilerParams(
            collective_id=collective_id, has_side_effects=True, vmem_limit_bytes=50 << 20
        ),
    )(part, normed, hidden, gain, column, score, inverse)


def attention_kernel(
    heads, q, g, kx, v, low, dq, dk, dv, qt, gt, ot, dqt, stat, sent, slots, send, recv
):
    me = lax.axis_index("ctx")
    length = q.shape[0]
    factor = HD**-0.5 * LOG2E

    def greet(d, _):
        signal({"ctx": (me + d) % CTX})
        return 0

    lax.fori_loop(1, CTX, greet, 0)
    pl.semaphore_wait(pltpu.get_barrier_semaphore(), CTX - 1)

    for h in range(heads):
        cols = slice(h * HD, (h + 1) * HD)
        qt[cols, :] = q[:, cols].T
        gt[cols, :] = g[:, cols].T
    key_id = lax.broadcasted_iota(jnp.int32, (length, length), 0)
    query_id = lax.broadcasted_iota(jnp.int32, (length, length), 1)
    low_v = low[0:1, :]

    def keep(j, diagonal):
        allowed = key_id >= low_v - j * length
        return allowed & (key_id <= query_id) if diagonal else allowed

    def forward(j, diagonal):
        key = kx[j, :length, :]
        value_t = v[j].T
        allowed = keep(j, diagonal)
        for h in range(heads):
            cols = slice(h * HD, (h + 1) * HD)
            logits = jnp.dot(key, qt[cols, :], preferred_element_type=jnp.float32) * factor
            logits = jnp.where(allowed, logits, NEG)
            top = jnp.max(logits, axis=0, keepdims=True)
            if diagonal:
                weights = jnp.exp2(logits - top)
                stat[h : h + 1, :] = top
                stat[8 + h : 9 + h, :] = jnp.sum(weights, axis=0, keepdims=True)
                ot[cols, :] = jnp.dot(
                    value_t, weights.astype(jnp.bfloat16), preferred_element_type=jnp.float32
                )
            else:
                old = stat[h : h + 1, :]
                top = jnp.maximum(old, top)
                weights = jnp.exp2(logits - top)
                shrink = jnp.exp2(old - top)
                stat[h : h + 1, :] = top
                stat[8 + h : 9 + h, :] = stat[8 + h : 9 + h, :] * shrink + jnp.sum(
                    weights, axis=0, keepdims=True
                )
                ot[cols, :] = ot[cols, :] * shrink + jnp.dot(
                    value_t, weights.astype(jnp.bfloat16), preferred_element_type=jnp.float32
                )

    forward(me, True)

    def forward_step(i, _):
        forward(me - i, False)
        return 0

    lax.fori_loop(1, me + 1, forward_step, 0)
    for h in range(heads):
        cols = slice(h * HD, (h + 1) * HD)
        total = stat[8 + h : 9 + h, :]
        delta = jnp.sum(ot[cols, :] * gt[cols, :].astype(jnp.float32), axis=0, keepdims=True)
        stat[16 + h : 17 + h, :] = delta / total
        stat[h : h + 1, :] = stat[h : h + 1, :] + jnp.log2(total)

    def backward(j, diagonal):
        key = kx[j, :length, :]
        key_t = key.T
        value = v[j]
        allowed = keep(j, diagonal)
        key_sum = jnp.zeros((length, HD), jnp.float32)
        value_sum = jnp.zeros((length, HD), jnp.float32)
        for h in range(heads):
            cols = slice(h * HD, (h + 1) * HD)
            logits = jnp.dot(key, qt[cols, :], preferred_element_type=jnp.float32) * factor
            logits = jnp.where(allowed, logits, NEG)
            prob = jnp.exp2(logits - stat[h : h + 1, :])
            prob_grad = jnp.dot(value, gt[cols, :], preferred_element_type=jnp.float32)
            logit_grad = (prob * (prob_grad - stat[16 + h : 17 + h, :])).astype(jnp.bfloat16)
            value_sum += jnp.dot(
                prob.astype(jnp.bfloat16), g[:, cols], preferred_element_type=jnp.float32
            )
            key_sum += jnp.dot(logit_grad, q[:, cols], preferred_element_type=jnp.float32)
            query_part = jnp.dot(key_t, logit_grad, preferred_element_type=jnp.float32)
            dqt[cols, :] = query_part if diagonal else dqt[cols, :] + query_part
        return key_sum, value_sum

    key_own, value_own = backward(me, True)
    dk[...] = key_own.astype(jnp.bfloat16)
    dv[...] = value_own.astype(jnp.bfloat16)
    sent[me, :length, :] = key_own.astype(jnp.bfloat16)
    sent[me, length:, :] = value_own.astype(jnp.bfloat16)

    def outgoing(j):
        return remote(sent.at[j], slots.at[me], send.at[j], recv.at[me], {"ctx": j})

    def backward_step(i, _):
        j = me - i
        key_part, value_part = backward(j, False)
        sent[j, :length, :] = key_part.astype(jnp.bfloat16)
        sent[j, length:, :] = value_part.astype(jnp.bfloat16)
        outgoing(j).start()
        return 0

    lax.fori_loop(1, me + 1, backward_step, 0)
    for h in range(heads):
        cols = slice(h * HD, (h + 1) * HD)
        dq[:, cols] = (dqt[cols, :].T * HD**-0.5).astype(jnp.bfloat16)

    def collect(j, total):
        remote(sent.at[me], slots.at[j], send.at[j], recv.at[j], {"ctx": j}).wait_recv()
        return total + slots[j].astype(jnp.float32)

    total = lax.fori_loop(me + 1, CTX, collect, sent[me].astype(jnp.float32))
    dk[...] = (total[:length] * HD**-0.5).astype(jnp.bfloat16)
    dv[...] = total[length:].astype(jnp.bfloat16)

    def drain(j, _):
        outgoing(j).wait_send()
        return 0

    lax.fori_loop(0, me, drain, 0)


def attention(q, g, kx, v, low, collective_id):
    length, width = q.shape
    return pl.pallas_call(
        functools.partial(attention_kernel, width // HD),
        out_shape=[
            jax.ShapeDtypeStruct((length, width), jnp.bfloat16),
            jax.ShapeDtypeStruct((length, HD), jnp.bfloat16),
            jax.ShapeDtypeStruct((length, HD), jnp.bfloat16),
        ],
        in_specs=[pl.BlockSpec(memory_space=pltpu.VMEM)] * 5,
        out_specs=[pl.BlockSpec(memory_space=pltpu.VMEM)] * 3,
        scratch_shapes=[
            pltpu.VMEM((width, length), jnp.bfloat16),
            pltpu.VMEM((width, length), jnp.bfloat16),
            pltpu.VMEM((width, length), jnp.float32),
            pltpu.VMEM((width, length), jnp.float32),
            pltpu.VMEM((24, length), jnp.float32),
            pltpu.VMEM((CTX, 2 * length, HD), jnp.bfloat16),
            pltpu.VMEM((CTX, 2 * length, HD), jnp.bfloat16),
            pltpu.SemaphoreType.DMA((CTX,)),
            pltpu.SemaphoreType.DMA((CTX,)),
        ],
        compiler_params=pltpu.CompilerParams(
            collective_id=collective_id, has_side_effects=True, vmem_limit_bytes=50 << 20
        ),
    )(q, g, kx, v, low)


def quarters(rows):
    return rows.reshape(-1, CAPL, 4, 1280).transpose(0, 2, 1, 3).reshape(-1, 16, 1280)


def whole(blocks):
    return blocks.reshape(-1, 4, CAPL, 1280).transpose(0, 2, 1, 3).reshape(-1, 5120)


def local(
    residual,
    out_grad,
    queries,
    key_rows,
    value_rows,
    doc_ids,
    expert_ids,
    norm_gain,
    router_columns,
    gate_weight,
    up_weight,
    down_weight,
    out_weight,
):
    ctx_index = lax.axis_index("ctx")
    tp_index = lax.axis_index("tp")
    length = residual.shape[0]
    mine = (expert_ids[None, :] == jnp.arange(TP)[:, None]).astype(jnp.int32)
    slot = jnp.cumsum(mine, axis=1) - mine
    place = ((mine[:, None, :] > 0) & (slot[:, None, :] == jnp.arange(CAPL)[None, :, None])).astype(
        jnp.bfloat16
    )
    own_place = lax.dynamic_index_in_dim(place, tp_index, 0, keepdims=False)
    rows_hidden = jnp.dot(own_place, residual, preferred_element_type=jnp.float32).astype(jnp.bfloat16)
    rows_grad = jnp.dot(own_place, out_grad, preferred_element_type=jnp.float32).astype(jnp.bfloat16)
    counts = jnp.sum(
        (doc_ids[None, :] < jnp.arange(16)[:, None]).astype(jnp.float32), axis=1, keepdims=True
    )
    key_ext = jnp.concatenate(
        [key_rows, jnp.broadcast_to(counts, (16, HD)).astype(jnp.bfloat16)], axis=0
    )
    weight_t = out_weight.T
    hidden_b, grad_b, key_all, value_all, weight_b, weight_a = gather(
        [
            quarters(rows_hidden)[0],
            quarters(rows_grad)[0],
            key_ext,
            value_rows,
            weight_t[:, 384:],
            weight_t[:, :384],
        ],
        [0, 1, 0, 1, 0, 1],
        1,
    )
    key_all = key_all.reshape(CTX, length + 16, HD)
    value_all = value_all.reshape(CTX, length, HD)
    weight_a = weight_a.reshape(-1, 384)
    weight_b = weight_b.reshape(-1, 256)
    all_hidden = whole(hidden_b.reshape(CTX, 16, 1280))
    all_grad = whole(grad_b.reshape(CTX, 16, 1280))
    gain = norm_gain.astype(jnp.float32)
    hidden_all = all_hidden.astype(jnp.float32)
    inverse = lax.rsqrt(jnp.mean(hidden_all * hidden_all, axis=1, keepdims=True) + EPS)
    normed = (hidden_all * inverse * gain).astype(jnp.bfloat16)
    column = router_columns[:, 0]
    score = jax.nn.sigmoid(jnp.dot(normed, column, preferred_element_type=jnp.float32))[:, None]
    routed = (normed.astype(jnp.float32) * score).astype(jnp.bfloat16)
    gate_local = gate_weight[0]
    up_local = up_weight[0]
    down_local = down_weight[0]
    gate = jnp.dot(routed, gate_local, preferred_element_type=jnp.float32)
    upward = jnp.dot(routed, up_local, preferred_element_type=jnp.float32)
    sigma = jax.nn.sigmoid(gate)
    swish = gate * sigma
    active = (swish * upward).astype(jnp.bfloat16)
    active_grad = contract(all_grad, down_local, 1, 1)
    gate_delta = (active_grad * upward * sigma * (1.0 + gate * (1.0 - sigma))).astype(jnp.bfloat16)
    up_delta = (active_grad * swish).astype(jnp.bfloat16)
    grad_down = contract(active, all_grad, 0, 0).astype(jnp.bfloat16)[None]
    grad_gate = contract(routed, gate_delta, 0, 0).astype(jnp.bfloat16)[None]
    grad_up = contract(routed, up_delta, 0, 0).astype(jnp.bfloat16)[None]
    part = contract(gate_delta, gate_local, 1, 1) + contract(up_delta, up_local, 1, 1)
    first_row = ctx_index * CAPL

    def own(array):
        return lax.dynamic_slice_in_dim(array, first_row, CAPL, 0)

    def wide(vector):
        return jnp.broadcast_to(vector.reshape(4, 1, 1280), (4, CAPL, 1280)).reshape(16, 1280)

    def tall(array):
        return jnp.broadcast_to(jnp.tile(own(array), (4, 1)), (16, 128))

    rows = expert_rows(
        quarters(part.astype(jnp.bfloat16)),
        quarters(own(normed))[0],
        quarters(own(all_hidden))[0],
        wide(gain),
        wide(column.astype(jnp.float32)),
        tall(score),
        tall(inverse),
        2,
    )
    rows_all = whole(rows)
    moe_grad = contract(place.reshape(16, length), rows_all, 0, 0)
    residual_grad = (out_grad.astype(jnp.float32) + moe_grad).astype(jnp.bfloat16)
    attn_grad = jnp.concatenate(
        [
            jnp.dot(residual_grad, weight_a, preferred_element_type=jnp.float32).astype(jnp.bfloat16),
            jnp.dot(residual_grad, weight_b, preferred_element_type=jnp.float32).astype(jnp.bfloat16),
        ],
        axis=1,
    )
    starts = jnp.sum(key_all[:, length : length + 8, 0].astype(jnp.float32), axis=0)
    low = jnp.sum(
        jnp.where(doc_ids[None, :] == jnp.arange(8)[:, None], starts[:, None], 0.0), axis=0
    ).astype(jnp.int32)
    low = jnp.broadcast_to(low[None, :], (8, length))
    query_grad, key_grad, value_grad = attention(queries, attn_grad, key_all, value_all, low, 3)
    return (residual_grad, query_grad, key_grad, value_grad, grad_gate, grad_up, grad_down)


def solution(mesh):
    in_specs = (
        P("ctx", None),
        P("ctx", None),
        P("ctx", "tp"),
        P("ctx", "tp"),
        P("ctx", "tp"),
        P("ctx"),
        P("ctx"),
        P(),
        P(None, "tp"),
        P("tp", None, "ctx"),
        P("tp", None, "ctx"),
        P("tp", "ctx", None),
        P("tp", "ctx"),
    )
    out_specs = (
        P("ctx", None),
        P("ctx", "tp"),
        P("ctx", "tp"),
        P("ctx", "tp"),
        P("tp", None, "ctx"),
        P("tp", None, "ctx"),
        P("tp", "ctx", None),
    )
    return jax.shard_map(local, mesh=mesh, in_specs=in_specs, out_specs=out_specs, check_vma=False)
```

time: 1900 us -> 301 us (0.16)
  waiting for transfers between devices: 1650 us -> 0 us
  Pallas kernels: 0 us -> 227 us
  blocking collectives: 82.7 us -> 0 us
  loops' own time: 63.8 us -> 0 us
  matrix products: 45.9 us -> 22.4 us
    all_gather x5 -> x0, waiting for transfers between devices: 774 us -> none  [the longest x1 170 us: local(): lax.all_gather(out_weight, 'ctx', axis=1, tiled=True)]
    reduce_scatter x2 -> x0, waiting for transfers between devices: 526 us -> none  [the longest x1 355 us: local(): lax.psum_scatter(key_acc, 'ctx', scatter_dimension=0, tiled=True)]
    unnamed x10 -> x0, waiting for transfers between devices: 323 us -> none
    pallas_call x0 -> x3, Pallas kernels: none -> 227 us  [the longest x1 113 us: attention(): pl.pallas_call(functools.partial(attention_kernel, width // HD), out_shap...]
    all_gather x1 -> x0, blocking collectives: 82.7 us -> none  [local(): lax.all_gather(doc_ids, 'ctx', axis=0, tiled=True)]
    another operation x34 -> x0, loops' own time: 63.8 us -> none  [the longest x2 63.3 us: sweep_keys(): return lax.fori_loop(0, count // width, advance, carry)]
    psum x1 -> x0, waiting for transfers between devices: 24.4 us -> none  [local(): moe_grad = lax.psum(token_part, 'tp')]
  transfers between devices with their start and end apart: 9 -> 0, of which waited for: 9 -> 0; matrix products, arithmetic and copies ran while one was open for 2% -> 0% of each run, Pallas kernels for 0% -> 0%
where the time goes in v1:
time: 301 us; the launch traced here: 299 us
  Pallas kernels  227 us (75%)
  local copies, waits for them, and re-layouts  35.3 us (12%)
  matrix products  22.4 us (7%)
  other arithmetic  13.5 us (4%)
    pallas_call x1, Pallas kernels, attention(): pl.pallas_call(functools.partial(attention_kernel, width // HD), out_shap...  113 us
    pallas_call x1, Pallas kernels, gather(): pl.pallas_call(functools.partial(gather_kernel, orders), out_shape=[jax.S...  88.4 us
    pallas_call x1, Pallas kernels, expert_rows(): pl.pallas_call(rows_kernel, out_shape=jax.ShapeDtypeStruct((TP, 16, 1280)...  25.6 us
    dot_general x7, matrix products, contract(): lax.dot_general(left, right, (((left_dim,), (right_dim,)), ((), ())), pre...  14.1 us
    unnamed x52, local copies, waits for them, and re-layouts  11.4 us
    another operation x4, local copies, waits for them, and re-layouts, whole(): blocks.reshape(-1, 4, CAPL, 1280).transpose(0, 2, 1, 3).reshape(-1, 5120)  10.8 us
    reshape x3, local copies, waits for them, and re-layouts, quarters(): rows.reshape(-1, CAPL, 4, 1280).transpose(0, 2, 1, 3).reshape(-1, 16, 1280)  9.95 us

profile of v1, /device:TPU:0, one launch (start us, length us, event | category | flops | bytes accessed | tf_op | source)
XLA Modules:
  0.0 299.3 jit_solution(1901745834249474327)
XLA Ops:
  0.6 0.8 compare_convert_fusion
  1.5 1.2 reduce-window.6
  3.1 0.7 convert_subtract_fusion
  3.8 0.7 convert_compare_fusion
  4.5 0.7 mul.79
  5.2 2.3 convolution_convert_fusion.4
  7.5 2.2 convolution_convert_fusion.3
  10.1 88.4 %shard_map.180 = (bf16[4,4,2,16,1280]{4,3,2,1,0:T(8,128)(2,1)S(1)}, bf16[4,4,2,16,1280]{4,3,2,1,0:T(8,128)(2,1)S(1)}, bf16[4,4,2,272,128]{4,3,2,1,0:T(8,128)(2,1...) custom-call(bf16[16,1280]{1,0:T(8,128)(2,1)S(1)} %squeeze_reshape.12, ...), custom_call_target="tpu_custom_call" | custom-call | tf_op jit(solution)/shard_map/pallas_call | solution.py:149
  98.5 1.0 copy-done.3
  99.5 1.1 copy-done.4
  100.6 3.5 %reshape_reshape.7 = bf16[32,4,4,1280]{3,2,1,0:T(4,128)(2,1)} reshape(bf16[4,4,2,16,1280]{4,3,2,1,0:T(8,128)(2,1)} %copy-done.4) | data formatting | bytes 2621440 | tf_op jit(solution)/shard_map/reshape;reshape | solution.py:416
  104.1 2.2 fusion.5
  106.3 2.1 fusion.7
  108.4 0.2 copy.47
  108.6 0.4 fusion.20
  109.2 2.5 multiply_convert_fusion.2
  111.7 0.2 copy.48
  111.9 0.5 fusion.10
  112.4 1.2 copy-done.11
  113.6 0.5 fusion.13
  114.1 3.5 %reshape_reshape.6 = bf16[32,4,4,1280]{3,2,1,0:T(4,128)(2,1)} reshape(bf16[4,4,2,16,1280]{4,3,2,1,0:T(8,128)(2,1)} %copy-done.3) | data formatting | bytes 2621440 | tf_op jit(solution)/shard_map/reshape;reshape | solution.py:416
  117.6 2.0 copy.39
  119.8 1.0 multiply_convert_fusion.6
  120.8 1.0 fusion.8
  121.8 0.7 copy-done.12
  122.5 2.0 fusion.4
  124.6 3.7 %reshape.266 = bf16[32,4,4,1280]{3,2,1,0:T(4,128)(2,1)} reshape(bf16[128,5120]{1,0:T(8,128)(2,1)} %fusion.4) | data formatting | bytes 2621440 | tf_op jit(solution)/shard_map/reshape | solution.py:412
  128.3 2.9 copy.57
  131.2 3.4 %reshape.267.part = bf16[32,16,1280]{2,1,0:T(8,128)(2,1)} reshape(bf16[32,4,4,1280]{3,2,1,0:T(4,128)(2,1)} %bitcast.118) | data formatting | bytes 2621440 | tf_op jit(solution)/shard_map/reshape | solution.py:412
  134.5 1.8 copy.40
  136.4 1.2 copy.49
  137.7 1.7 multiply_convert_fusion.1
  139.4 1.0 constant_dynamic-slice_fusion.1
  141.3 1.3 copy-done.1
  142.6 25.6 %shard_map.181 = bf16[4,16,1280]{2,1,0:T(8,128)(2,1)S(1)} custom-call(bf16[32,16,1280]{2,1,0:T(8,128)(2,1)S(1)} %copy-done.1, bf16[16,1280]{1,0:T(8,128)(2,1)S(1)} %squeeze_reshape.14.normed, bf16[16,1280]{1,0:T(8,128)(2,1)S(1)} %squeeze_reshape.15.hidden, f32[16,1280]{1,0:T(8,128)S(1)} %reshape.271.gain, f32[16,1280]{1,0:T(8,128)S(1)} %reshape.272.column, ...), custom_call_target="tpu_custom_call" | custom-call | tf_op jit(solution)/shard_map/pallas_call | solution.py:236
  168.4 2.8 fusion
  171.2 0.8 convolution_convert_fusion.6
  172.1 0.6 copy-done.14
  172.7 1.6 copy-done.20
  174.3 1.5 convolution_convert_fusion.5
  175.9 1.1 convert_reduce_fusion
  177.1 112.9 %shard_map.182 = (bf16[256,640]{1,0:T(8,128)(2,1)S(1)}, bf16[256,128]{1,0:T(8,128)(2,1)S(1)}, bf16[256,128]{1,0:T(8,128)(2,1)S(1)}) custom-call(bf16[256,640]{1,0:T(8,128)(2,1)S(1)} %copy-done.5, bf16[256,640]{1,0:T(8,128)(2,1)S(1)} %pad_maximum_fusion.g, bf16[32,272,128]{2,1,0:T(8,128)(2,1)} %bitcast.122, bf16[32,256,128]{2,1,0:T(8,128)(2,1)S(1)} %bitcast.108, ...), custom_call_target="tpu_custom_call" | custom-call | tf_op jit(solution)/shard_map/pallas_call | solution.py:385
  290.0 2.5 fusion.1
  292.5 2.4 fusion.2
  294.9 2.4 fusion.3
  297.3 0.7 copy.61
  298.1 0.6 copy.62
  298.7 0.6 copy.63
  (81 shorter events, 2.3 us)
Async XLA Ops:
  0.6 111.2 %copy-start = (bf16[1,5120,256]{2,1,0:T(8,128)(2,1)S(1)}, bf16[1,5120,256]{2,1,0:T(8,128)(2,1)}, u32[]{:S(2)}) copy-start(bf16[1,5120,256]{2,1,0:T(8,128)(2,1)} %param.22) | copy-start | bytes 7864324
  5.2 4.6 %copy-start.19 = (s32[256]{0:T(256)S(1)}, s32[256]{0:T(256)}, u32[]{:S(2)}) copy-start(s32[256]{0:T(256)} %param.18) | copy-start | bytes 3076
  5.2 4.7 %copy-start.17 = (bf16[256,128]{1,0:T(8,128)(2,1)S(1)}, bf16[256,128]{1,0:T(8,128)(2,1)}, u32[]{:S(2)}) copy-start(bf16[256,128]{1,0:T(8,128)(2,1)} %param.16) | copy-start | bytes 196612
  5.2 4.8 %copy-start.15 = (bf16[640,160]{0,1:T(8,128)(2,1)S(1)}, bf16[640,160]{0,1:T(8,128)(2,1)}, u32[]{:S(2)}) copy-start(bf16[640,160]{0,1:T(8,128)(2,1)} %param.25) | copy-start | bytes 614404
  5.2 4.8 %copy-start.6 = (bf16[256,128]{1,0:T(8,128)(2,1)S(1)}, bf16[256,128]{1,0:T(8,128)(2,1)}, u32[]{:S(2)}) copy-start(bf16[256,128]{1,0:T(8,128)(2,1)} %refs_3_.1) | copy-start | bytes 196612
  98.5 1.1 copy-start.3
  99.5 1.1 copy-start.4
  106.3 2.3 copy-start.16
  111.8 1.7 copy-start.11
  117.6 2.2 copy-start.13
  119.7 2.0 copy-start.9
  120.8 1.7 copy-start.12
  134.5 3.1 %copy-start.18 = (bf16[5120]{0:T(1024)(128)(2,1)S(1)}, bf16[5120]{0:T(1024)(128)(2,1)}, u32[]{:S(2)}) copy-start(bf16[5120]{0:T(1024)(128)(2,1)} %param.20) | copy-start | bytes 30724
  139.4 1.1 copy-start.7
  141.3 1.3 copy-start.1
  168.4 2.8 copy-start.21
  171.2 1.5 copy-start.14
  171.2 3.1 %copy-start.20 = (bf16[4,4,2,160,384]{4,3,2,1,0:T(8,128)(2,1)S(1)}, bf16[4,4,2,160,384]{4,3,2,1,0:T(8,128)(2,1)}, u32[]{:S(2)}) copy-start(bf16[4,4,2,160,384]{4,3,2,1,0:T(8,128)(2,1)} %get-tuple-element.18) | copy-start | bytes 11796484
  174.3 2.8 copy-start.2
  174.3 2.8 copy-start.5
  175.9 114.2 %copy-start.8 = (bf16[128,5120]{1,0:T(8,128)(2,1)S(1)}, bf16[128,5120]{1,0:T(8,128)(2,1)}, u32[]{:S(2)}) copy-start(bf16[128,5120]{1,0:T(8,128)(2,1)} %copy-done.7) | copy-start | bytes 3932164
  292.5 2.5 copy-start.10

commit v2 on v1

v2 whole, which is shorter than its diff:
```python
import jax
import jax.numpy as jnp
from jax import lax
from jax.experimental import pallas as pl
from jax.experimental.pallas import tpu as pltpu
from jax.sharding import PartitionSpec as P

HD = 128
CAPL = 4
EPS = 1e-05
NEG = -1e30
LOG2E = 1.4426950408889634
MESH = pl.DeviceIdType.MESH
NY, NZ, NX = 4, 4, 2
CTX = NY * NZ * NX
TP = 4


def contract(left, right, left_dim, right_dim):
    return lax.dot_general(
        left, right, (((left_dim,), (right_dim,)), ((), ())), preferred_element_type=jnp.float32
    )


def place_of():
    me = lax.axis_index("ctx")
    return me // (NZ * NX), (me // NX) % NZ, me % NX


def at(y, z, x):
    return {"ctx": y * (NZ * NX) + z * NX + x}


def signal(device):
    pl.semaphore_signal(
        pltpu.get_barrier_semaphore(), inc=1, device_id=device, device_id_type=MESH
    )


def remote(src, dst, send, recv, device):
    return pltpu.make_async_remote_copy(
        src_ref=src, dst_ref=dst, send_sem=send, recv_sem=recv, device_id=device, device_id_type=MESH
    )


class Gather:
    def __init__(self, src, buf, order, send, recv, local):
        self.src, self.buf, self.order = src, buf, order
        self.send, self.recv, self.local = send, recv, local

    def copy(self, src, dst, k, device):
        return remote(src, dst, self.send.at[k], self.recv.at[k], device)

    def along_z(self, step):
        return (self.order == 0) == (step in (2, 3))

    def slab(self, step, offset, half):
        y, z, x = place_of()
        buf = self.buf
        if self.along_z(step):
            z = (z + offset) % NZ
        else:
            y = (y + offset) % NY
        if step in (2, 3):
            return buf.at[y, z] if half is None else buf.at[y, z, half]
        if self.along_z(step):
            return buf.at[:, z] if half is None else buf.at[2 * half : 2 * half + 2, z]
        return buf.at[y] if half is None else buf.at[y, 2 * half : 2 * half + 2]

    def device(self, step, offset):
        y, z, x = place_of()
        if self.along_z(step):
            return at(y, (z + offset) % NZ, x)
        return at((y + offset) % NY, z, x)

    def sends(self, step):
        y, z, x = place_of()
        if step == 1:
            return [self.copy(self.src, self.buf.at[y, z, x], 0, at(y, z, 1 - x))]
        copies = []
        for i, d in enumerate((1, 3)):
            k = 1 + 2 * (step - 2) + i
            part = self.slab(step, 0, None) if step in (2, 4) else self.slab(step, 4 - d, i)
            copies.append(self.copy(part, part, k, self.device(step, d)))
        return copies

    def receives(self, step):
        y, z, x = place_of()
        if step == 1:
            part = self.buf.at[y, z, 1 - x]
            return [self.copy(part, part, 0, at(y, z, 1 - x))]
        copies = []
        for i, d in enumerate((1, 3)):
            k = 1 + 2 * (step - 2) + i
            part = self.slab(step, 4 - d, None) if step in (2, 4) else self.slab(step, 2, i)
            copies.append(self.copy(part, part, k, self.device(step, d)))
        return copies

    def own(self):
        y, z, x = place_of()
        return pltpu.make_async_copy(self.src, self.buf.at[y, z, x], self.local)

    def start(self, step):
        if step == 1:
            self.own().start()
        for copy in self.sends(step):
            copy.start()

    def arrive(self, step):
        if step == 1:
            self.own().wait()
        for copy in self.receives(step):
            copy.wait_recv()

    def finish(self):
        for step in range(1, 6):
            for copy in self.sends(step):
                copy.wait_send()


BIG = 2.0**60


def fold_rows(column):
    row = lax.broadcasted_iota(jnp.int32, (16, 16), 0) & (CAPL - 1)
    col = lax.broadcasted_iota(jnp.int32, (16, 16), 1) & (CAPL - 1)
    same = (row == col).astype(jnp.float32)
    wide = jnp.broadcast_to(column, (16, 128))
    return jnp.dot(
        same, wide, precision=lax.Precision.HIGHEST, preferred_element_type=jnp.float32
    )[:, :1]


def dot(left, right):
    return jnp.dot(left, right, preferred_element_type=jnp.float32)


def split3(value):
    high = value.astype(jnp.bfloat16).astype(jnp.float32)
    rest = value - high
    middle = rest.astype(jnp.bfloat16).astype(jnp.float32)
    return high, middle, rest - middle


def kernel(
    hid, grd, kx, v, wb, wa, q, doc, gain, column, gain16, column16, scat,
    gate_hbm, up_hbm, down_hbm, og_hbm,
    res_out, routed_out, grads_out, gd_out, ud_out, act_out, dq, dk, dv,
    hbuf, gbuf, kbuf, vbuf, wbbuf, wabuf, gu, down, og, res, perm, perm_t, hx, grads, routed,
    gd, ud, act, stack, part, slots, rows, kxe, vxe, qx, gx, ot, top, sb, pb, lb, qs, gs, dqt,
    acc, dslots,
    gsend, grecv, glocal, send, recv, tsend, trecv, dsend, drecv, loads, stores,
):
    me = lax.axis_index("ctx")
    tp = lax.axis_index("tp")
    length = q.shape[0]
    heads = q.shape[1] // HD
    scale = HD**-0.5
    factor = scale * LOG2E
    features = down.shape[1]

    fetch_gate = pltpu.make_async_copy(gate_hbm, gu.at[:features], loads.at[0])
    fetch_up = pltpu.make_async_copy(up_hbm, gu.at[features:], loads.at[1])
    fetch_down = pltpu.make_async_copy(down_hbm, down, loads.at[2])
    fetch_og = pltpu.make_async_copy(og_hbm, og, loads.at[3])
    fetch_gate.start()
    fetch_up.start()
    fetch_down.start()
    fetch_og.start()

    def greet(d, _):
        signal({"ctx": (me + d) % CTX})
        return 0

    lax.fori_loop(1, CTX, greet, 0)
    for d in range(1, TP):
        signal({"tp": (tp + d) % TP})
    pl.semaphore_wait(pltpu.get_barrier_semaphore(), CTX - 1 + TP - 1)

    def piece(src, buf, order, i):
        return Gather(src, buf, order, gsend.at[i], grecv.at[i], glocal.at[i])

    moe = [piece(hid, hbuf, 0, 0), piece(grd, gbuf, 1, 1)]
    keys = [piece(kx, kbuf, 0, 2), piece(v, vbuf, 1, 3)]
    weights = [piece(wb, wbbuf, 0, 4), piece(wa, wabuf, 1, 5)]

    def go(parts, step):
        for part in parts:
            if step > 1:
                part.arrive(step - 1)
            if step < 6:
                part.start(step)

    go(moe, 1)
    go(keys, 1)
    go(weights, 1)
    go(moe, 2)
    go(moe, 3)

    def row_of(index):
        token = index & 127
        return (token >> 2) * 16 + (index >> 7) * 4 + (token & 3)

    a = lax.broadcasted_iota(jnp.int32, (512, 512), 0)
    b = lax.broadcasted_iota(jnp.int32, (512, 512), 1)
    perm[...] = (a == row_of(b)).astype(jnp.float32).astype(jnp.bfloat16)
    perm_t[...] = (b == row_of(a)).astype(jnp.float32).astype(jnp.bfloat16)
    for h in range(heads):
        cols = slice(h * HD, (h + 1) * HD)
        qs[h * length : (h + 1) * length, :] = q[:, cols]
        qx[h, :HD, :] = q[:, cols].T
        qx[h, HD:, :] = jnp.zeros((HD, length), jnp.bfloat16)
        gx[h, HD:, :] = jnp.zeros((HD, length), jnp.bfloat16)

    go(keys, 2)
    go(moe, 4)
    go(weights, 2)
    go(keys, 3)
    go(moe, 5)
    go(weights, 3)
    go(keys, 4)
    go(moe, 6)

    quarter = features // 4

    def unfold(t, _):
        cols = pl.ds(pl.multiple_of(t * 256, 256), 256)
        block = hbuf[:, :, :, :, cols].reshape(512, 256)
        hx[:, cols] = dot(perm_t[...], block).astype(jnp.bfloat16)
        block = gbuf[:, :, :, :, cols].reshape(512, 256)
        values = dot(perm_t[...], block).astype(jnp.bfloat16)
        for i in range(4):
            grads[:, pl.ds(pl.multiple_of(i * quarter + t * 256, 256), 256)] = values[
                i * 128 : (i + 1) * 128
            ]
        return 0

    lax.fori_loop(0, quarter // 256, unfold, 0)
    total = jnp.zeros((128, 1), jnp.float32)
    for i in range(4):
        x = hx[i * 128 : (i + 1) * 128, :].astype(jnp.float32)
        total += jnp.sum(x * x, axis=1, keepdims=True)
    inverse = lax.rsqrt(total * (1.0 / features) + EPS)
    total = jnp.zeros((128, 1), jnp.float32)
    for i in range(4):
        cols = slice(i * quarter, (i + 1) * quarter)
        x = hx[i * 128 : (i + 1) * 128, :].astype(jnp.float32)
        normed = (x * inverse * gain[:, cols]).astype(jnp.bfloat16)
        routed[:, cols] = normed
        total += jnp.sum(normed.astype(jnp.float32) * column[:, cols], axis=1, keepdims=True)
    score = jax.nn.sigmoid(total)
    for i in range(4):
        cols = slice(i * quarter, (i + 1) * quarter)
        routed[:, cols] = (routed[:, cols].astype(jnp.float32) * score).astype(jnp.bfloat16)
    go(keys, 5)
    fetch_gate.wait()
    fetch_up.wait()
    fetch_down.wait()
    gate = dot(routed[...], gu[:features, :])
    upward = dot(routed[...], gu[features:, :])
    active_grad = contract(grads[...], down[...], 1, 1)
    sigma = jax.nn.sigmoid(gate)
    swish = gate * sigma
    act[...] = (swish * upward).astype(jnp.bfloat16)
    gd[...] = (active_grad * upward * sigma * (1.0 + gate * (1.0 - sigma))).astype(jnp.bfloat16)
    ud[...] = (active_grad * swish).astype(jnp.bfloat16)

    def back(t, _):
        first = pl.multiple_of(t * 640, 640)
        values = contract(gd[...], gu[pl.ds(first, 640), :], 1, 1)
        values += contract(ud[...], gu[pl.ds(features + first, 640), :], 1, 1)
        line = pl.multiple_of((t // 2) * 128, 128)
        stack[pl.ds(line, 128), pl.ds(pl.multiple_of((t % 2) * 640, 640), 640)] = values.astype(
            jnp.bfloat16
        )
        return 0

    lax.fori_loop(0, 8, back, 0)

    def fold(t, _):
        cols = pl.ds(pl.multiple_of(t * 256, 256), 256)
        part[:, :, cols] = dot(perm[...], stack[:, cols]).astype(jnp.bfloat16).reshape(CTX, 16, 256)
        return 0

    lax.fori_loop(0, quarter // 256, fold, 0)

    def partial(d):
        to = (me + d) % CTX
        return remote(part.at[to], slots.at[me], send.at[d], recv.at[d], {"ctx": to})

    def launch(d, _):
        partial(d).start()
        return 0

    lax.fori_loop(1, CTX, launch, 0)
    saves = [
        pltpu.make_async_copy(src, dst, stores.at[i])
        for i, (src, dst) in enumerate(
            [(routed, routed_out), (grads, grads_out), (gd, gd_out), (ud, ud_out), (act, act_out)]
        )
    ]
    for save in saves:
        save.start()
    go(weights, 4)
    go(keys, 6)

    counts = jnp.sum(kbuf[:, :, :, length:, :].astype(jnp.float32), axis=(0, 1, 2))[:8]
    a = lax.broadcasted_iota(jnp.int32, (8, HD), 0)
    b = lax.broadcasted_iota(jnp.int32, (8, HD), 1)
    starts = jnp.sum(jnp.where(a == b, counts, 0.0), axis=0, keepdims=True)
    ends = jnp.sum(jnp.where(a == b + 1, counts, 0.0), axis=0, keepdims=True)
    lane = lax.broadcasted_iota(jnp.int32, (1, HD), 1)
    ends = jnp.where(lane == 7, float(CTX * length), ends)
    token = lax.broadcasted_iota(jnp.int32, (length, HD), 0).astype(jnp.float32)
    ones_at = (lane >= 8) & (lane < 11)
    ones_row = jnp.where(ones_at, 1.0, 0.0)
    ones_block = jnp.broadcast_to(ones_row, (length, HD)).astype(jnp.bfloat16)

    def extend(j, _):
        y, z, x = j // (NZ * NX), (j // NX) % NZ, j % NX
        lines = pl.ds(pl.multiple_of(j * length, length), length)
        first = (j * length).astype(jnp.float32)
        inside = (token >= starts - first) & (token < ends - first)
        kxe[lines, :HD] = kbuf[y, z, x, :length, :]
        kxe[lines, HD:] = jnp.where(inside, -BIG, ones_row).astype(jnp.bfloat16)
        vxe[lines, :HD] = vbuf[y, z, x]
        vxe[lines, HD:] = ones_block
        return 0

    lax.fori_loop(0, me + 1, extend, 0)
    row16 = lax.broadcasted_iota(jnp.int32, (16, length), 0)
    other = jnp.where((row16 < 8) & (row16 != doc[...]), 1.0, 0.0)
    for h in range(heads):
        qx[h, HD : HD + 16, :] = other.astype(jnp.bfloat16)
    key_id = lax.broadcasted_iota(jnp.int32, (length, length), 0)
    query_id = lax.broadcasted_iota(jnp.int32, (length, length), 1)
    ones16 = jnp.ones((16, length), jnp.bfloat16)

    def forward(j, diagonal):
        lines = pl.ds(pl.multiple_of(j * length, length), length)
        key = kxe[lines, :]
        value_t = jnp.concatenate([vxe[lines, :HD].T, ones16], axis=0)
        tops, shrinks = [], []
        for h in range(heads):
            logits = dot(key, qx[h])
            if diagonal:
                logits = jnp.where(key_id <= query_id, logits, -BIG)
            sb[:, h * length : (h + 1) * length] = logits
            new = jnp.max(logits, axis=0, keepdims=True)
            if not diagonal:
                old = top[h]
                new = jnp.maximum(old, new)
                shrinks.append(jnp.exp2((old - new) * factor))
            top[h] = new
            tops.append(new * factor)
        for h in range(heads):
            cols = slice(h * length, (h + 1) * length)
            pb[:, cols] = jnp.exp2(sb[:, cols] * factor - tops[h]).astype(jnp.bfloat16)
        for h in range(heads):
            more = dot(value_t, pb[:, h * length : (h + 1) * length])
            ot[h] = more if diagonal else ot[h] * shrinks[h] + more

    def forward_step(i, _):
        forward(me - i, False)
        return 0

    forward(me, True)
    half = (me + 1) // 2
    lax.fori_loop(1, half, forward_step, 0)
    go(weights, 5)
    lax.fori_loop(jnp.maximum(half, 1), me + 1, forward_step, 0)

    def collect(d, sums):
        source = (me + CTX - d) % CTX
        remote(part.at[me], slots.at[source], send.at[d], recv.at[d], {"ctx": source}).wait_recv()
        return sums + slots[source].astype(jnp.float32)

    routed_grad = lax.fori_loop(1, CTX, collect, part[me].astype(jnp.float32))
    hidden = hid[...].astype(jnp.float32)
    inverse = lax.rsqrt(
        fold_rows(jnp.sum(hidden * hidden, axis=1, keepdims=True)) * (1.0 / features) + EPS
    )
    normed = (hidden * inverse * gain16[...]).astype(jnp.bfloat16).astype(jnp.float32)
    score = jax.nn.sigmoid(fold_rows(jnp.sum(normed * column16[...], axis=1, keepdims=True)))
    dots = fold_rows(jnp.sum(routed_grad * normed, axis=1, keepdims=True))
    score_grad = dots * score * (1.0 - score)
    scaled = gain16[...] * (routed_grad * score + score_grad * column16[...])
    mean = fold_rows(jnp.sum(scaled * hidden, axis=1, keepdims=True)) * (1.0 / features)
    own_rows = inverse * scaled - hidden * (inverse * inverse * inverse) * mean
    rows[tp] = own_rows.astype(jnp.bfloat16)

    def swap(d, source):
        return remote(
            rows.at[source], rows.at[source], tsend.at[d], trecv.at[d], {"tp": (tp + d) % TP}
        )

    for d in range(1, TP):
        swap(d, tp).start()
    fetch_og.wait()
    for d in range(1, TP):
        swap(d, (tp + TP - d) % TP).wait_recv()

    for i in range(4):

        def add(t, _, i=i):
            cols = pl.ds(pl.multiple_of(t * 256, 256), 256)
            wide = pl.ds(pl.multiple_of(i * quarter + t * 256, 256), 256)
            more = dot(scat[i], rows[:, :, cols].reshape(TP * 16, 256))
            res[:, wide] = (og[:, wide].astype(jnp.float32) + more).astype(jnp.bfloat16)
            return 0

        lax.fori_loop(0, quarter // 256, add, 0)
    save_res = pltpu.make_async_copy(res, res_out, stores.at[5])
    save_res.start()

    go(weights, 6)
    acc[...] = jnp.zeros_like(acc)

    def project(i, _):
        y, z = i // 2, (i % 2) * 2
        left = res[:, pl.ds(pl.multiple_of(i * 640, 640), 640)]
        acc[:, :384] += dot(left, wabuf[y, pl.ds(z, 2)].reshape(640, 384))
        acc[:, 384:] += dot(left, wbbuf[y, pl.ds(z, 2)].reshape(640, 256))
        return 0

    lax.fori_loop(0, 8, project, 0)
    for h in range(heads):
        grad = acc[:, h * HD : (h + 1) * HD].astype(jnp.bfloat16)
        gs[h * length : (h + 1) * length, :] = grad
        grad_t = grad.T
        gx[h, :HD, :] = grad_t
        total = ot[h, HD : HD + 1, :]
        delta = jnp.sum(ot[h, :HD, :] * grad_t.astype(jnp.float32), axis=0, keepdims=True) / total
        high, middle, rest = split3(-delta)
        extra = jnp.where(row16 == 8, high, 0.0)
        extra = jnp.where(row16 == 9, middle, extra)
        extra = jnp.where(row16 == 10, rest, extra)
        gx[h, HD : HD + 16, :] = extra.astype(jnp.bfloat16)
        high, middle, rest = split3(-(top[h] + jnp.log2(total) * (1.0 / factor)))
        extra = jnp.where(row16 == 8, high, other)
        extra = jnp.where(row16 == 9, middle, extra)
        extra = jnp.where(row16 == 10, rest, extra)
        qx[h, HD : HD + 16, :] = extra.astype(jnp.bfloat16)

    def backward(j, diagonal):
        lines = pl.ds(pl.multiple_of(j * length, length), length)
        key = kxe[lines, :]
        key_t = kxe[lines, :HD].T
        value = vxe[lines, :]
        for h in range(heads):
            cols = slice(h * length, (h + 1) * length)
            logits = dot(key, qx[h])
            if diagonal:
                logits = jnp.where(key_id <= query_id, logits, -BIG)
            prob = jnp.exp2(logits * factor)
            lb[:, cols] = (prob * dot(value, gx[h])).astype(jnp.bfloat16)
            pb[:, cols] = prob.astype(jnp.bfloat16)
        value_sum = dot(pb[...], gs[...])
        key_sum = dot(lb[...], qs[...]) * scale
        for h in range(heads):
            more = dot(key_t, lb[:, h * length : (h + 1) * length])
            dqt[h] = more if diagonal else dqt[h] + more
        gu[lines, :HD] = key_sum.astype(jnp.bfloat16)
        gu[lines, HD:] = value_sum.astype(jnp.bfloat16)

    def outgoing(j):
        lines = pl.ds(pl.multiple_of(j * length, length), length)
        return remote(gu.at[lines], dslots.at[me], dsend.at[j], drecv.at[me], {"ctx": j})

    def backward_step(i, _):
        backward(me - i, False)
        outgoing(me - i).start()
        return 0

    backward(me, True)
    lax.fori_loop(1, me + 1, backward_step, 0)
    for h in range(heads):
        dq[:, h * HD : (h + 1) * HD] = (dqt[h].T * scale).astype(jnp.bfloat16)
    own = pl.ds(pl.multiple_of(me * length, length), length)

    def gather_sums(j, sums):
        remote(gu.at[own], dslots.at[j], dsend.at[j], drecv.at[j], {"ctx": j}).wait_recv()
        return sums + dslots[j].astype(jnp.float32)

    total = lax.fori_loop(me + 1, CTX, gather_sums, gu[own, :].astype(jnp.float32))
    dk[...] = total[:, :HD].astype(jnp.bfloat16)
    dv[...] = total[:, HD:].astype(jnp.bfloat16)

    def drain(j, _):
        outgoing(j).wait_send()
        return 0

    lax.fori_loop(0, me, drain, 0)

    def drain_partial(d, _):
        partial(d).wait_send()
        return 0

    lax.fori_loop(1, CTX, drain_partial, 0)
    for d in range(1, TP):
        swap(d, tp).wait_send()
    for piece_ in moe + keys + weights:
        piece_.finish()
    for save in saves:
        save.wait()
    save_res.wait()


def fused(hid, grd, kx, v, wb, wa, q, doc, gain, column, gain16, column16, scat, gate, up, down, og):
    length, width = q.shape
    heads = width // HD
    features = down.shape[1]
    rows = CTX * CAPL
    hidden = gate.shape[1]
    bf16, f32 = jnp.bfloat16, jnp.float32

    def shape(*dims):
        return jax.ShapeDtypeStruct(dims, bf16)

    vmem = pl.BlockSpec(memory_space=pltpu.VMEM)
    hbm = pl.BlockSpec(memory_space=pl.ANY)
    return pl.pallas_call(
        kernel,
        out_shape=[
            shape(length, features),
            shape(rows, features),
            shape(rows, features),
            shape(rows, hidden),
            shape(rows, hidden),
            shape(rows, hidden),
            shape(length, width),
            shape(length, HD),
            shape(length, HD),
        ],
        in_specs=[vmem] * 13 + [hbm] * 4,
        out_specs=[hbm] * 6 + [vmem] * 3,
        scratch_shapes=[
            pltpu.VMEM((NY, NZ, NX) + hid.shape, bf16),
            pltpu.VMEM((NY, NZ, NX) + grd.shape, bf16),
            pltpu.VMEM((NY, NZ, NX) + kx.shape, bf16),
            pltpu.VMEM((NY, NZ, NX) + v.shape, bf16),
            pltpu.VMEM((NY, NZ, NX) + wb.shape, bf16),
            pltpu.VMEM((NY, NZ, NX) + wa.shape, bf16),
            pltpu.VMEM((2 * features, hidden), bf16),
            pltpu.VMEM((hidden, features), bf16),
            pltpu.VMEM((length, features), bf16),
            pltpu.VMEM((length, features), bf16),
            pltpu.VMEM((512, 512), bf16),
            pltpu.VMEM((512, 512), bf16),
            pltpu.VMEM((512, features // 4), bf16),
            pltpu.VMEM((rows, features), bf16),
            pltpu.VMEM((rows, features), bf16),
            pltpu.VMEM((rows, hidden), bf16),
            pltpu.VMEM((rows, hidden), bf16),
            pltpu.VMEM((rows, hidden), bf16),
            pltpu.VMEM((512, features // 4), bf16),
            pltpu.VMEM((CTX, 16, features // 4), bf16),
            pltpu.VMEM((CTX, 16, features // 4), bf16),
            pltpu.VMEM((TP, 16, features // 4), bf16),
            pltpu.VMEM((CTX * length, 2 * HD), bf16),
            pltpu.VMEM((CTX * length, 2 * HD), bf16),
            pltpu.VMEM((heads, 2 * HD, length), bf16),
            pltpu.VMEM((heads, 2 * HD, length), bf16),
            pltpu.VMEM((heads, HD + 16, length), f32),
            pltpu.VMEM((heads, 1, length), f32),
            pltpu.VMEM((length, heads * length), f32),
            pltpu.VMEM((length, heads * length), bf16),
            pltpu.VMEM((length, heads * length), bf16),
            pltpu.VMEM((heads * length, HD), bf16),
            pltpu.VMEM((heads * length, HD), bf16),
            pltpu.VMEM((heads, HD, length), f32),
            pltpu.VMEM((length, width), f32),
            pltpu.VMEM((CTX, length, 2 * HD), bf16),
            pltpu.SemaphoreType.DMA((6, 9)),
            pltpu.SemaphoreType.DMA((6, 9)),
            pltpu.SemaphoreType.DMA((6,)),
            pltpu.SemaphoreType.DMA((CTX,)),
            pltpu.SemaphoreType.DMA((CTX,)),
            pltpu.SemaphoreType.DMA((TP,)),
            pltpu.SemaphoreType.DMA((TP,)),
            pltpu.SemaphoreType.DMA((CTX,)),
            pltpu.SemaphoreType.DMA((CTX,)),
            pltpu.SemaphoreType.DMA((4,)),
            pltpu.SemaphoreType.DMA((6,)),
        ],
        compiler_params=pltpu.CompilerParams(
            collective_id=1, has_side_effects=True, vmem_limit_bytes=60 << 20
        ),
    )(hid, grd, kx, v, wb, wa, q, doc, gain, column, gain16, column16, scat, gate, up, down, og)


def quarters(rows):
    return rows.reshape(CAPL, 4, -1).transpose(1, 0, 2).reshape(16, -1)


def local(
    residual,
    out_grad,
    queries,
    key_rows,
    value_rows,
    doc_ids,
    expert_ids,
    norm_gain,
    router_columns,
    gate_weight,
    up_weight,
    down_weight,
    out_weight,
):
    tp_index = lax.axis_index("tp")
    length = residual.shape[0]
    mine = (expert_ids[None, :] == jnp.arange(TP)[:, None]).astype(jnp.int32)
    slot = jnp.cumsum(mine, axis=1) - mine
    place = ((mine[:, None, :] > 0) & (slot[:, None, :] == jnp.arange(CAPL)[None, :, None])).astype(
        jnp.bfloat16
    )
    own_place = lax.dynamic_index_in_dim(place, tp_index, 0, keepdims=False)
    rows_hidden = dot(own_place, residual).astype(jnp.bfloat16)
    rows_grad = dot(own_place, out_grad).astype(jnp.bfloat16)
    scat = (
        place.transpose(2, 0, 1)[None, :, :, None, :]
        * jnp.eye(4, dtype=jnp.bfloat16)[:, None, None, :, None]
    ).reshape(4, length, TP * 16)
    counts = jnp.sum(
        (doc_ids[None, :] < jnp.arange(16)[:, None]).astype(jnp.float32), axis=1, keepdims=True
    )
    key_ext = jnp.concatenate(
        [key_rows, jnp.broadcast_to(counts, (16, HD)).astype(jnp.bfloat16)], axis=0
    )
    weight_t = out_weight.T
    gain = norm_gain.astype(jnp.float32)
    column = router_columns[:, 0].astype(jnp.float32)

    def wide(vector):
        return jnp.broadcast_to(vector.reshape(4, 1, -1), (4, CAPL, vector.size // 4)).reshape(16, -1)

    residual_grad, routed, grads, gate_delta, up_delta, active, query_grad, key_grad, value_grad = fused(
        quarters(rows_hidden),
        quarters(rows_grad),
        key_ext,
        value_rows,
        weight_t[:, 384:],
        weight_t[:, :384],
        queries,
        doc_ids[None, :],
        gain[None, :],
        column[None, :],
        wide(gain),
        wide(column),
        scat,
        gate_weight[0],
        up_weight[0],
        down_weight[0],
        out_grad,
    )
    grad_down = contract(active, grads, 0, 0).astype(jnp.bfloat16)[None]
    grad_gate = contract(routed, gate_delta, 0, 0).astype(jnp.bfloat16)[None]
    grad_up = contract(routed, up_delta, 0, 0).astype(jnp.bfloat16)[None]
    return (residual_grad, query_grad, key_grad, value_grad, grad_gate, grad_up, grad_down)


def solution(mesh):
    in_specs = (
        P("ctx", None),
        P("ctx", None),
        P("ctx", "tp"),
        P("ctx", "tp"),
        P("ctx", "tp"),
        P("ctx"),
        P("ctx"),
        P(),
        P(None, "tp"),
        P("tp", None, "ctx"),
        P("tp", None, "ctx"),
        P("tp", "ctx", None),
        P("tp", "ctx"),
    )
    out_specs = (
        P("ctx", None),
        P("ctx", "tp"),
        P("ctx", "tp"),
        P("ctx", "tp"),
        P("tp", None, "ctx"),
        P("tp", None, "ctx"),
        P("tp", "ctx", None),
    )
    return jax.shard_map(local, mesh=mesh, in_specs=in_specs, out_specs=out_specs, check_vma=False)
```

time: 301 us -> 218 us (0.72)
  Pallas kernels: 227 us -> 185 us
  local copies, waits for them, and re-layouts: 35.3 us -> 8.83 us
  matrix products: 22.4 us -> 11.2 us
    pallas_call x3 -> x1, Pallas kernels: 227 us -> 185 us  [fused(): pl.pallas_call(kernel, out_shape=[shape(length, features), shape(rows, fe...]
    another operation x16 -> x2, local copies, waits for them, and re-layouts: 11.3 us -> 0.1 us  [the longest x4 10.8 us: whole(): blocks.reshape(-1, 4, CAPL, 1280).transpose(0, 2, 1, 3).reshape(-1, 5120)]
    unnamed x52 -> x26, local copies, waits for them, and re-layouts: 11.4 us -> 3.53 us
    reshape x7 -> x4, local copies, waits for them, and re-layouts: 10.1 us -> 2.62 us  [the longest x2 1.33 us: wide(): jnp.broadcast_to(vector.reshape(4, 1, -1), (4, CAPL, vector.size // 4))]
    dot_general x7 -> x2, matrix products: 8.3 us -> 2.68 us  [dot(): return jnp.dot(left, right, preferred_element_type=jnp.float32)]
    dot_general x7 -> x3, matrix products: 14.1 us -> 8.52 us  [contract(): lax.dot_general(left, right, (((left_dim,), (right_dim,)), ((), ())), pre...]
    convert_element_type x5 -> x4, other arithmetic: 6.34 us -> 2.15 us  [the longest x2 2.13 us: local(): column = router_columns[:, 0].astype(jnp.float32)]
    reduce_sum x3 -> x0, other arithmetic: 3.4 us -> none  [the longest x1 2.23 us: local(): jnp.mean(hidden_all * hidden_all, axis=1, keepdims=True) + EPS]
where the time goes in v2:
time: 218 us; the launch traced here: 217 us
  Pallas kernels  185 us (85%)
  matrix products  11.2 us (5%)
  other arithmetic  10.6 us (5%)
  local copies, waits for them, and re-layouts  8.83 us (4%)
    pallas_call x1, Pallas kernels, fused(): pl.pallas_call(kernel, out_shape=[shape(length, features), shape(rows, fe...  185 us
    dot_general x3, matrix products, contract(): lax.dot_general(left, right, (((left_dim,), (right_dim,)), ((), ())), pre...  8.52 us

profile of v2, /device:TPU:0, one launch (start us, length us, event | category | flops | bytes accessed | tf_op | source)
XLA Modules:
  0.0 216.8 jit_solution(12862029311657082)
XLA Ops:
  0.6 0.0 copy-start
  0.7 0.9 convert_reduce_fusion.1
  1.6 0.7 convert_compare_fusion
  2.3 0.7 convert_compare_fusion.1
  3.0 0.7 compare_convert_fusion
  3.7 1.2 reduce-window.6
  4.9 0.1 slice.16
  5.0 0.1 copy.30
  5.1 0.1 copy.31
  5.2 0.1 add_bitcast_fusion
  5.3 0.7 fusion.22
  6.0 0.7 convert_subtract_fusion
  6.7 0.1 mul.25
  6.8 0.1 mul.26
  6.9 0.7 broadcast_in_dim.21
  7.6 1.3 convert_element_type.84
  8.9 0.8 convert_reduce_fusion
  9.7 1.4 convert_bitcast_fusion.column
  11.1 0.1 copy.34
  11.2 0.0 copy-start.8
  11.2 0.0 copy-start.5
  11.2 2.2 %convolution_convert_fusion.3 = bf16[4,5120]{1,0:T(4,128)(2,1)S(1)} fusion(bf16[256,5120]{1,0:T(8,128)(2,1)} %og_hbm.1, s32[1,256]{1,0:T(1,128)S(1)} %constant_dynamic-slice_fusion, pred[1,256]{1,0:T(4,128)(4,1)S(1)} %constant_dynamic-slice_fusion.1), kind=kOutput, calls=%fused_computation.6 | convolution fusion | flops 10508288 | bytes 2663680 | tf_op jit(solution)/shard_map/dot_general | solution.py:135
  13.4 0.6 reshape.138.grd
  14.1 0.0 copy-done
  14.1 0.4 convolution_convert_fusion.4
  14.5 0.6 reshape.136.hid
  15.2 0.7 reshape.140.column16
  15.9 0.7 reshape.139.gain16
  16.5 0.0 copy-done.8
  16.5 0.7 pad_maximum_fusion.kx
  17.3 0.0 copy-done.5
  17.3 0.6 slice.17.wb
  17.9 0.7 slice.18.wa
  18.6 0.7 broadcast_multiply_fusion.scat
  19.3 185.4 %shard_map.180 = (bf16[256,5120]{1,0:T(8,128)(2,1)}, bf16[128,5120]{1,0:T(8,128)(2,1)}, bf16[128,5120]{1,0:T(8,128)(2,1)}, bf16[128,256]{1,0:T(8,128)(2,1)}, bf1...) custom-call(bf16[16,1280]{1,0:T(8,128)(2,1)} %reshape.136.hid, ...), custom_call_target="tpu_custom_call" | custom-call | tf_op jit(solution)/shard_map/pallas_call | solution.py:522
  204.7 0.0 copy-start.1
  204.7 0.0 copy-start.7
  204.7 3.8 %fusion = bf16[1,5120,256]{2,1,0:T(8,128)(2,1)} fusion(bf16[128,5120]{1,0:T(8,128)(2,1)} %get-tuple-element.20, bf16[128,256]{1,0:T(8,128)(2,1)} %get-tuple-element.21), kind=kOutput, calls=%fused_computation.3 | convolution fusion | flops 336855040 | bytes 3997696 | tf_op jit(solution)/shard_map/dot_general | solution.py:20
  208.5 0.0 copy-done.1
  208.5 0.0 copy-done.7
  208.5 0.0 copy-start.6
  208.5 2.4 %fusion.1 = bf16[1,5120,256]{2,1,0:T(8,128)(2,1)} fusion(bf16[128,5120]{1,0:T(8,128)(2,1)S(1)} %copy-done.1, bf16[128,256]{1,0:T(8,128)(2,1)S(1)} %copy-done.7), kind=kOutput, calls=%fused_computation.4 | convolution fusion | flops 336855040 | bytes 3997696 | tf_op jit(solution)/shard_map/dot_general | solution.py:20
  210.9 2.4 %fusion.2 = bf16[1,256,5120]{2,1,0:T(8,128)(2,1)} fusion(bf16[128,256]{1,0:T(8,128)(2,1)S(1)} %copy-done.6, bf16[128,5120]{1,0:T(8,128)(2,1)S(1)} %copy-done.3), kind=kOutput, calls=%fused_computation.5 | convolution fusion | flops 336855040 | bytes 3997696 | tf_op jit(solution)/shard_map/dot_general | solution.py:20
  213.3 1.5 copy.43
  214.8 0.7 copy.44
  215.5 0.0 copy-done.10
  215.5 0.6 copy.45
  216.1 0.6 copy.46
  (22 shorter events, 0.2 us)
Async XLA Ops:
  0.6 13.5 %copy-start = (bf16[256,5120]{1,0:T(8,128)(2,1)S(1)}, bf16[256,5120]{1,0:T(8,128)(2,1)}, u32[]{:S(2)}) copy-start(bf16[256,5120]{1,0:T(8,128)(2,1)} %param.13) | copy-start | bytes 7864324
  11.2 5.4 %copy-start.8 = (bf16[256,128]{1,0:T(8,128)(2,1)S(1)}, bf16[256,128]{1,0:T(8,128)(2,1)}, u32[]{:S(2)}) copy-start(bf16[256,128]{1,0:T(8,128)(2,1)} %param.16) | copy-start | bytes 196612
  11.2 6.1 %copy-start.5 = (bf16[640,160]{0,1:T(8,128)(2,1)S(1)}, bf16[640,160]{0,1:T(8,128)(2,1)}, u32[]{:S(2)}) copy-start(bf16[640,160]{0,1:T(8,128)(2,1)} %param.25) | copy-start | bytes 614404
  204.7 3.8 %copy-start.1 = (bf16[128,5120]{1,0:T(8,128)(2,1)S(1)}, bf16[128,5120]{1,0:T(8,128)(2,1)}, u32[]{:S(2)}) copy-start(bf16[128,5120]{1,0:T(8,128)(2,1)} %get-tuple-element.20) | copy-start | bytes 3932164
  204.7 3.8 %copy-start.7 = (bf16[128,256]{1,0:T(8,128)(2,1)S(1)}, bf16[128,256]{1,0:T(8,128)(2,1)}, u32[]{:S(2)}) copy-start(bf16[128,256]{1,0:T(8,128)(2,1)} %get-tuple-element.22) | copy-start | bytes 196612
  208.5 2.4 %copy-start.3 = (bf16[128,5120]{1,0:T(8,128)(2,1)S(1)}, bf16[128,5120]{1,0:T(8,128)(2,1)}, u32[]{:S(2)}) copy-start(bf16[128,5120]{1,0:T(8,128)(2,1)} %get-tuple-element.24) | copy-start | bytes 3932164
  208.5 2.4 %copy-start.6 = (bf16[128,256]{1,0:T(8,128)(2,1)S(1)}, bf16[128,256]{1,0:T(8,128)(2,1)}, u32[]{:S(2)}) copy-start(bf16[128,256]{1,0:T(8,128)(2,1)} %get-tuple-element.23) | copy-start | bytes 196612
  210.9 2.4 %copy-start.2 = (bf16[256,5120]{1,0:T(8,128)(2,1)S(1)}, bf16[256,5120]{1,0:T(8,128)(2,1)}, u32[]{:S(2)}) copy-start(bf16[256,5120]{1,0:T(8,128)(2,1)} %get-tuple-element.32) | copy-start | bytes 7864324
  213.3 1.5 copy-start.4
  213.3 2.2 %copy-start.10 = (bf16[256,128]{1,0:T(8,128)(2,1)S(1)}, bf16[256,128]{1,0:T(8,128)(2,1)}, u32[]{:S(2)}) copy-start(bf16[256,128]{1,0:T(8,128)(2,1)} %get-tuple-element.34) | copy-start | bytes 196612
  213.3 2.9 %copy-start.9 = (bf16[256,128]{1,0:T(8,128)(2,1)S(1)}, bf16[256,128]{1,0:T(8,128)(2,1)}, u32[]{:S(2)}) copy-start(bf16[256,128]{1,0:T(8,128)(2,1)} %get-tuple-element.35) | copy-start | bytes 196612

commit v3 on v2

--- a/solution.py
+++ b/solution.py
@@ -118,6 +118,88 @@
                 copy.wait_send()
 
 
+class Scatter:
+    def __init__(self, p, a1, c1, a2, c2, order, send, recv):
+        self.p, self.order, self.send, self.recv = p, order, send, recv
+        self.far_in, self.near_in = (a1, a2), (c1, c2)
+
+    def along_z(self, stage):
+        return (self.order == 0) == (stage == 2)
+
+    def slab(self, stage, offset, half):
+        y, z, x = place_of()
+        p = self.p
+        if self.along_z(stage):
+            z = (z + offset) % NZ
+        else:
+            y = (y + offset) % NY
+        if stage == 2:
+            return p.at[y, z] if half is None else p.at[y, z, half : half + 1]
+        if self.along_z(stage):
+            return p.at[:, z] if half is None else p.at[2 * half : 2 * half + 2, z]
+        return p.at[y] if half is None else p.at[y, 2 * half : 2 * half + 2]
+
+    def device(self, stage, offset):
+        y, z, x = place_of()
+        if self.along_z(stage):
+            return at(y, (z + offset) % NZ, x)
+        return at((y + offset) % NY, z, x)
+
+    def copies(self, stage, near):
+        result = []
+        for i, d in enumerate((1, 3)):
+            k = 4 * (stage - 1) + 2 * near + i
+            if near:
+                src, dst = self.slab(stage, d, None), self.near_in[stage - 1].at[i]
+            else:
+                src, dst = self.slab(stage, 2, i), self.far_in[stage - 1].at[i]
+            result.append(remote(src, dst, self.send.at[k], self.recv.at[k], self.device(stage, d)))
+        return result
+
+    def far(self, stage):
+        for copy in self.copies(stage, 0):
+            copy.start()
+
+    def near(self, stage):
+        for i, (d, copy) in enumerate(zip((1, 3), self.copies(stage, 0))):
+            copy.wait_recv()
+            half = self.slab(stage, d, i)
+            more = self.far_in[stage - 1][i].astype(jnp.float32)
+            half[...] = (half[...].astype(jnp.float32) + more).astype(jnp.bfloat16)
+        for copy in self.copies(stage, 1):
+            copy.start()
+
+    def own(self, stage):
+        for copy in self.copies(stage, 1):
+            copy.wait_recv()
+        slab = self.slab(stage, 0, None)
+        arrived = self.near_in[stage - 1]
+        more = arrived[0].astype(jnp.float32) + arrived[1].astype(jnp.float32)
+        slab[...] = (slab[...].astype(jnp.float32) + more).astype(jnp.bfloat16)
+
+    def swap(self):
+        y, z, x = place_of()
+        there = self.far_in[1].at[2]
+        return remote(
+            self.p.at[y, z, 1 - x], there.at[0], self.send.at[8], self.recv.at[8], at(y, z, 1 - x)
+        )
+
+    def last(self):
+        self.swap().start()
+
+    def total(self):
+        y, z, x = place_of()
+        self.swap().wait_recv()
+        return self.p[y, z, x].astype(jnp.float32) + self.far_in[1][2, 0].astype(jnp.float32)
+
+    def finish(self):
+        for stage in (1, 2):
+            for near in (0, 1):
+                for copy in self.copies(stage, near):
+                    copy.wait_send()
+        self.swap().wait_send()
+
+
 BIG = 2.0**60
 
 
@@ -143,12 +225,11 @@
 
 
 def kernel(
-    hid, grd, kx, v, wb, wa, q, doc, gain, column, gain16, column16, scat,
-    gate_hbm, up_hbm, down_hbm, og_hbm,
+    kin, v, wt, q, doc, eid, gain, column, gate_hbm, up_hbm, down_hbm, og_hbm, residual_hbm,
     res_out, routed_out, grads_out, gd_out, ud_out, act_out, dq, dk, dv,
     hbuf, gbuf, kbuf, vbuf, wbbuf, wabuf, gu, down, og, res, perm, perm_t, hx, grads, routed,
-    gd, ud, act, stack, part, slots, rows, kxe, vxe, qx, gx, ot, top, sb, pb, lb, qs, gs, dqt,
-    acc, dslots,
+    gd, ud, act, part, slots, rows, kxe, vxe, qx, gx, ot, top, sb, pb, lb, qs, gs, dqt,
+    acc, hid, grd, kx, scat, gain16, column16, pk, pv, ak, ck, bk, ek, av, cv, bv, ev,
     gsend, grecv, glocal, send, recv, tsend, trecv, dsend, drecv, loads, stores,
 ):
     me = lax.axis_index("ctx")
@@ -163,10 +244,12 @@
     fetch_up = pltpu.make_async_copy(up_hbm, gu.at[features:], loads.at[1])
     fetch_down = pltpu.make_async_copy(down_hbm, down, loads.at[2])
     fetch_og = pltpu.make_async_copy(og_hbm, og, loads.at[3])
+    fetch_residual = pltpu.make_async_copy(residual_hbm, res, loads.at[4])
+    fetch_residual.start()
+    fetch_og.start()
     fetch_gate.start()
     fetch_up.start()
     fetch_down.start()
-    fetch_og.start()
 
     def greet(d, _):
         signal({"ctx": (me + d) % CTX})
@@ -175,6 +258,30 @@
     lax.fori_loop(1, CTX, greet, 0)
     for d in range(1, TP):
         signal({"tp": (tp + d) % TP})
+
+    quarter = features // 4
+    row16 = lax.broadcasted_iota(jnp.int32, (16, length), 0)
+    a = lax.broadcasted_iota(jnp.int32, (length, length), 0)
+    b = lax.broadcasted_iota(jnp.int32, (length, length), 1)
+    before = (a < b).astype(jnp.float32).astype(jnp.bfloat16)
+
+    def in_slot(expert, slot):
+        named = jnp.where(eid[...] == expert, 1.0, 0.0)
+        rank = dot(named.astype(jnp.bfloat16), before)
+        return jnp.where(rank == slot.astype(jnp.float32), named, 0.0)
+
+    mine = in_slot(jnp.broadcast_to(tp, (16, length)), row16 & (CAPL - 1))
+    kx[:length, :] = kin[...]
+    counts = jnp.sum(jnp.where(doc[...] < row16, 1.0, 0.0), axis=1, keepdims=True)
+    kx[length:, :] = jnp.broadcast_to(counts, (16, HD)).astype(jnp.bfloat16)
+    fetch_residual.wait()
+    fetch_og.wait()
+    for src, dst in ((res, hid), (og, grd)):
+        picked = jnp.zeros((16, quarter), jnp.float32)
+        for i in range(4):
+            take = jnp.where((row16 >> 2) == i, mine, 0.0).astype(jnp.bfloat16)
+            picked += dot(take, src[:, i * quarter : (i + 1) * quarter])
+        dst[...] = picked.astype(jnp.bfloat16)
     pl.semaphore_wait(pltpu.get_barrier_semaphore(), CTX - 1 + TP - 1)
 
     def piece(src, buf, order, i):
@@ -182,7 +289,7 @@
 
     moe = [piece(hid, hbuf, 0, 0), piece(grd, gbuf, 1, 1)]
     keys = [piece(kx, kbuf, 0, 2), piece(v, vbuf, 1, 3)]
-    weights = [piece(wb, wbbuf, 0, 4), piece(wa, wabuf, 1, 5)]
+    weights = [piece(wt.at[:, 384:], wbbuf, 0, 4), piece(wt.at[:, :384], wabuf, 1, 5)]
 
     def go(parts, step):
         for part in parts:
@@ -205,6 +312,16 @@
     b = lax.broadcasted_iota(jnp.int32, (512, 512), 1)
     perm[...] = (a == row_of(b)).astype(jnp.float32).astype(jnp.bfloat16)
     perm_t[...] = (b == row_of(a)).astype(jnp.float32).astype(jnp.bfloat16)
+    row64 = lax.broadcasted_iota(jnp.int32, (64, length), 0)
+    placed = in_slot(row64 >> 4, row64 & (CAPL - 1))
+    wide16 = lax.broadcasted_iota(jnp.int32, (16, quarter), 0) >> 2
+    gain16[...] = jnp.zeros_like(gain16)
+    column16[...] = jnp.zeros_like(column16)
+    for i in range(4):
+        cols = slice(i * quarter, (i + 1) * quarter)
+        gain16[...] += jnp.where(wide16 == i, gain[:, cols].astype(jnp.float32), 0.0)
+        column16[...] += jnp.where(wide16 == i, column[:, cols].astype(jnp.float32), 0.0)
+        scat[i] = jnp.where(((row64 >> 2) & 3) == i, placed, 0.0).T.astype(jnp.bfloat16)
     for h in range(heads):
         cols = slice(h * HD, (h + 1) * HD)
         qs[h * length : (h + 1) * length, :] = q[:, cols]
@@ -221,7 +338,6 @@
     go(keys, 4)
     go(moe, 6)
 
-    quarter = features // 4
 
     def unfold(t, _):
         cols = pl.ds(pl.multiple_of(t * 256, 256), 256)
@@ -245,9 +361,9 @@
     for i in range(4):
         cols = slice(i * quarter, (i + 1) * quarter)
         x = hx[i * 128 : (i + 1) * 128, :].astype(jnp.float32)
-        normed = (x * inverse * gain[:, cols]).astype(jnp.bfloat16)
+        normed = (x * inverse * gain[:, cols].astype(jnp.float32)).astype(jnp.bfloat16)
         routed[:, cols] = normed
-        total += jnp.sum(normed.astype(jnp.float32) * column[:, cols], axis=1, keepdims=True)
+        total += jnp.sum(normed.astype(jnp.float32) * column[:, cols].astype(jnp.float32), axis=1, keepdims=True)
     score = jax.nn.sigmoid(total)
     for i in range(4):
         cols = slice(i * quarter, (i + 1) * quarter)
@@ -270,7 +386,7 @@
         values = contract(gd[...], gu[pl.ds(first, 640), :], 1, 1)
         values += contract(ud[...], gu[pl.ds(features + first, 640), :], 1, 1)
         line = pl.multiple_of((t // 2) * 128, 128)
-        stack[pl.ds(line, 128), pl.ds(pl.multiple_of((t % 2) * 640, 640), 640)] = values.astype(
+        hx[pl.ds(line, 128), pl.ds(pl.multiple_of((t % 2) * 640, 640), 640)] = values.astype(
             jnp.bfloat16
         )
         return 0
@@ -279,7 +395,7 @@
 
     def fold(t, _):
         cols = pl.ds(pl.multiple_of(t * 256, 256), 256)
-        part[:, :, cols] = dot(perm[...], stack[:, cols]).astype(jnp.bfloat16).reshape(CTX, 16, 256)
+        part[:, :, cols] = dot(perm[...], hx[:, cols]).astype(jnp.bfloat16).reshape(CTX, 16, 256)
         return 0
 
     lax.fori_loop(0, quarter // 256, fold, 0)
@@ -328,7 +444,6 @@
         return 0
 
     lax.fori_loop(0, me + 1, extend, 0)
-    row16 = lax.broadcasted_iota(jnp.int32, (16, length), 0)
     other = jnp.where((row16 < 8) & (row16 != doc[...]), 1.0, 0.0)
     for h in range(heads):
         qx[h, HD : HD + 16, :] = other.astype(jnp.bfloat16)
@@ -396,7 +511,6 @@
 
     for d in range(1, TP):
         swap(d, tp).start()
-    fetch_og.wait()
     for d in range(1, TP):
         swap(d, (tp + TP - d) % TP).wait_recv()
 
@@ -459,38 +573,75 @@
         key_sum = dot(lb[...], qs[...]) * scale
         for h in range(heads):
             more = dot(key_t, lb[:, h * length : (h + 1) * length])
-            dqt[h] = more if diagonal else dqt[h] + more
-        gu[lines, :HD] = key_sum.astype(jnp.bfloat16)
-        gu[lines, HD:] = value_sum.astype(jnp.bfloat16)
-
-    def outgoing(j):
-        lines = pl.ds(pl.multiple_of(j * length, length), length)
-        return remote(gu.at[lines], dslots.at[me], dsend.at[j], drecv.at[me], {"ctx": j})
+            dqt[h] = dqt[h] + more
+        y, z, x = j // (NZ * NX), (j // NX) % NZ, j % NX
+        pk[y, z, x] = key_sum.astype(jnp.bfloat16)
+        pv[y, z, x] = value_sum.astype(jnp.bfloat16)
+
+    sums = [
+        Scatter(pk, ak, ck, bk, ek, 0, dsend.at[0], drecv.at[0]),
+        Scatter(pv, av, cv, bv, ev, 1, dsend.at[1], drecv.at[1]),
+    ]
+    y, z, x = place_of()
+    for h in range(heads):
+        dqt[h] = jnp.zeros((HD, length), jnp.float32)
 
     def backward_step(i, _):
-        backward(me - i, False)
-        outgoing(me - i).start()
-        return 0
-
-    backward(me, True)
-    lax.fori_loop(1, me + 1, backward_step, 0)
+        r = jnp.where(i < 14, i - 8, i - 14)
+        turn = jnp.where(i < 14, r // 2, r // 6)
+        to_y = (y + 3 - 2 * turn + turn // 2) % NY
+        turn = (r % 6) // 2
+        to_z = (z + 3 - 2 * turn + turn // 2) % NZ
+        to_y = jnp.where(i < 8, (y + 2) % NY, to_y)
+        to_z = jnp.where(i < 8, i // 2, jnp.where(i < 14, (z + 2) % NZ, to_z))
+        j = to_y * (NZ * NX) + to_z * NX + i % 2
+
+        @pl.when(j < me)
+        def _():
+            backward(j, False)
+
+        @pl.when(j == me)
+        def _():
+            backward(j, True)
+
+        @pl.when(j > me)
+        def _():
+            pk[to_y, to_z, i % 2] = jnp.zeros((length, HD), jnp.bfloat16)
+            pv[to_y, to_z, i % 2] = jnp.zeros((length, HD), jnp.bfloat16)
+
+        @pl.when(i == 7)
+        def _():
+            sums[0].far(1)
+
+        @pl.when(i == 13)
+        def _():
+            sums[1].far(1)
+
+        @pl.when(i == 25)
+        def _():
+            sums[0].near(1)
+
+        @pl.when(i == 29)
+        def _():
+            sums[1].near(1)
+
+        return 0
+
+    lax.fori_loop(0, CTX, backward_step, 0)
+    for part_ in sums:
+        part_.own(1)
+        part_.far(2)
     for h in range(heads):
         dq[:, h * HD : (h + 1) * HD] = (dqt[h].T * scale).astype(jnp.bfloat16)
-    own = pl.ds(pl.multiple_of(me * length, length), length)
-
-    def gather_sums(j, sums):
-        remote(gu.at[own], dslots.at[j], dsend.at[j], drecv.at[j], {"ctx": j}).wait_recv()
-        return sums + dslots[j].astype(jnp.float32)
-
-    total = lax.fori_loop(me + 1, CTX, gather_sums, gu[own, :].astype(jnp.float32))
-    dk[...] = total[:, :HD].astype(jnp.bfloat16)
-    dv[...] = total[:, HD:].astype(jnp.bfloat16)
-
-    def drain(j, _):
-        outgoing(j).wait_send()
-        return 0
-
-    lax.fori_loop(0, me, drain, 0)
+    for part_ in sums:
+        part_.near(2)
+    for part_ in sums:
+        part_.own(2)
+        part_.last()
+    dk[...] = sums[0].total().astype(jnp.bfloat16)
+    dv[...] = sums[1].total().astype(jnp.bfloat16)
+    for part_ in sums:
+        part_.finish()
 
     def drain_partial(d, _):
         partial(d).wait_send()
@@ -506,7 +657,7 @@
     save_res.wait()
 
 
-def fused(hid, grd, kx, v, wb, wa, q, doc, gain, column, gain16, column16, scat, gate, up, down, og):
+def fused(kin, v, wt, q, doc, eid, gain, column, gate, up, down, og, residual):
     length, width = q.shape
     heads = width // HD
     features = down.shape[1]
@@ -532,15 +683,15 @@
             shape(length, HD),
             shape(length, HD),
         ],
-        in_specs=[vmem] * 13 + [hbm] * 4,
+        in_specs=[vmem] * 8 + [hbm] * 5,
         out_specs=[hbm] * 6 + [vmem] * 3,
         scratch_shapes=[
-            pltpu.VMEM((NY, NZ, NX) + hid.shape, bf16),
-            pltpu.VMEM((NY, NZ, NX) + grd.shape, bf16),
-            pltpu.VMEM((NY, NZ, NX) + kx.shape, bf16),
+            pltpu.VMEM((NY, NZ, NX) + (16, features // 4), bf16),
+            pltpu.VMEM((NY, NZ, NX) + (16, features // 4), bf16),
+            pltpu.VMEM((NY, NZ, NX) + (length + 16, HD), bf16),
             pltpu.VMEM((NY, NZ, NX) + v.shape, bf16),
-            pltpu.VMEM((NY, NZ, NX) + wb.shape, bf16),
-            pltpu.VMEM((NY, NZ, NX) + wa.shape, bf16),
+            pltpu.VMEM((NY, NZ, NX) + (wt.shape[0], 256), bf16),
+            pltpu.VMEM((NY, NZ, NX) + (wt.shape[0], 384), bf16),
             pltpu.VMEM((2 * features, hidden), bf16),
             pltpu.VMEM((hidden, features), bf16),
             pltpu.VMEM((length, features), bf16),
@@ -553,7 +704,6 @@
             pltpu.VMEM((rows, hidden), bf16),
             pltpu.VMEM((rows, hidden), bf16),
             pltpu.VMEM((rows, hidden), bf16),
-            pltpu.VMEM((512, features // 4), bf16),
             pltpu.VMEM((CTX, 16, features // 4), bf16),
             pltpu.VMEM((CTX, 16, features // 4), bf16),
             pltpu.VMEM((TP, 16, features // 4), bf16),
@@ -570,7 +720,22 @@
             pltpu.VMEM((heads * length, HD), bf16),
             pltpu.VMEM((heads, HD, length), f32),
             pltpu.VMEM((length, width), f32),
-            pltpu.VMEM((CTX, length, 2 * HD), bf16),
+            pltpu.VMEM((16, features // 4), bf16),
+            pltpu.VMEM((16, features // 4), bf16),
+            pltpu.VMEM((length + 16, HD), bf16),
+            pltpu.VMEM((4, length, 64), bf16),
+            pltpu.VMEM((16, features // 4), f32),
+            pltpu.VMEM((16, features // 4), f32),
+            pltpu.VMEM((NY, NZ, NX, length, HD), bf16),
+            pltpu.VMEM((NY, NZ, NX, length, HD), bf16),
+            pltpu.VMEM((2, 2, 2, length, HD), bf16),
+            pltpu.VMEM((2, 4, 2, length, HD), bf16),
+            pltpu.VMEM((3, 1, length, HD), bf16),
+            pltpu.VMEM((2, 2, length, HD), bf16),
+            pltpu.VMEM((2, 2, 2, length, HD), bf16),
+            pltpu.VMEM((2, 4, 2, length, HD), bf16),
+            pltpu.VMEM((3, 1, length, HD), bf16),
+            pltpu.VMEM((2, 2, length, HD), bf16),
             pltpu.SemaphoreType.DMA((6, 9)),
             pltpu.SemaphoreType.DMA((6, 9)),
             pltpu.SemaphoreType.DMA((6,)),
@@ -578,19 +743,41 @@
             pltpu.SemaphoreType.DMA((CTX,)),
             pltpu.SemaphoreType.DMA((TP,)),
             pltpu.SemaphoreType.DMA((TP,)),
-            pltpu.SemaphoreType.DMA((CTX,)),
-            pltpu.SemaphoreType.DMA((CTX,)),
-            pltpu.SemaphoreType.DMA((4,)),
+            pltpu.SemaphoreType.DMA((2, 9)),
+            pltpu.SemaphoreType.DMA((2, 9)),
+            pltpu.SemaphoreType.DMA((5,)),
             pltpu.SemaphoreType.DMA((6,)),
         ],
         compiler_params=pltpu.CompilerParams(
             collective_id=1, has_side_effects=True, vmem_limit_bytes=60 << 20
         ),
-    )(hid, grd, kx, v, wb, wa, q, doc, gain, column, gain16, column16, scat, gate, up, down, og)
-
-
-def quarters(rows):
-    return rows.reshape(CAPL, 4, -1).transpose(1, 0, 2).reshape(16, -1)
+    )(kin, v, wt, q, doc, eid, gain, column, gate, up, down, og, residual)
+
+
+def products_kernel(routed, grads, gd, ud, act, gate, up, down):
+    gate[...] = contract(routed[...], gd[...], 0, 0).astype(jnp.bfloat16)
+    up[...] = contract(routed[...], ud[...], 0, 0).astype(jnp.bfloat16)
+    down[...] = contract(act[...], grads[...], 0, 0).astype(jnp.bfloat16)
+
+
+def products(routed, grads, gd, ud, act):
+    rows, features = routed.shape
+    hidden = gd.shape[1]
+    width = 512
+    tall = pl.BlockSpec((width, hidden), lambda i: (i, 0))
+    wide = pl.BlockSpec((rows, width), lambda i: (0, i))
+    fixed = pl.BlockSpec((rows, hidden), lambda i: (0, 0))
+    return pl.pallas_call(
+        products_kernel,
+        grid=(features // width,),
+        out_shape=[
+            jax.ShapeDtypeStruct((features, hidden), jnp.bfloat16),
+            jax.ShapeDtypeStruct((features, hidden), jnp.bfloat16),
+            jax.ShapeDtypeStruct((hidden, features), jnp.bfloat16),
+        ],
+        in_specs=[wide, wide, fixed, fixed, fixed],
+        out_specs=[tall, tall, pl.BlockSpec((hidden, width), lambda i: (0, i))],
+    )(routed, grads, gd, ud, act)
 
 
 def local(
@@ -608,56 +795,25 @@
     down_weight,
     out_weight,
 ):
-    tp_index = lax.axis_index("tp")
-    length = residual.shape[0]
-    mine = (expert_ids[None, :] == jnp.arange(TP)[:, None]).astype(jnp.int32)
-    slot = jnp.cumsum(mine, axis=1) - mine
-    place = ((mine[:, None, :] > 0) & (slot[:, None, :] == jnp.arange(CAPL)[None, :, None])).astype(
-        jnp.bfloat16
-    )
-    own_place = lax.dynamic_index_in_dim(place, tp_index, 0, keepdims=False)
-    rows_hidden = dot(own_place, residual).astype(jnp.bfloat16)
-    rows_grad = dot(own_place, out_grad).astype(jnp.bfloat16)
-    scat = (
-        place.transpose(2, 0, 1)[None, :, :, None, :]
-        * jnp.eye(4, dtype=jnp.bfloat16)[:, None, None, :, None]
-    ).reshape(4, length, TP * 16)
-    counts = jnp.sum(
-        (doc_ids[None, :] < jnp.arange(16)[:, None]).astype(jnp.float32), axis=1, keepdims=True
-    )
-    key_ext = jnp.concatenate(
-        [key_rows, jnp.broadcast_to(counts, (16, HD)).astype(jnp.bfloat16)], axis=0
-    )
-    weight_t = out_weight.T
-    gain = norm_gain.astype(jnp.float32)
-    column = router_columns[:, 0].astype(jnp.float32)
-
-    def wide(vector):
-        return jnp.broadcast_to(vector.reshape(4, 1, -1), (4, CAPL, vector.size // 4)).reshape(16, -1)
-
     residual_grad, routed, grads, gate_delta, up_delta, active, query_grad, key_grad, value_grad = fused(
-        quarters(rows_hidden),
-        quarters(rows_grad),
-        key_ext,
+        key_rows,
         value_rows,
-        weight_t[:, 384:],
-        weight_t[:, :384],
+        out_weight.T,
         queries,
         doc_ids[None, :],
-        gain[None, :],
-        column[None, :],
-        wide(gain),
-        wide(column),
-        scat,
+        expert_ids[None, :],
+        norm_gain[None, :],
+        router_columns.reshape(1, -1),
         gate_weight[0],
         up_weight[0],
         down_weight[0],
         out_grad,
+        residual,
     )
-    grad_down = contract(active, grads, 0, 0).astype(jnp.bfloat16)[None]
-    grad_gate = contract(routed, gate_delta, 0, 0).astype(jnp.bfloat16)[None]
-    grad_up = contract(routed, up_delta, 0, 0).astype(jnp.bfloat16)[None]
-    return (residual_grad, query_grad, key_grad, value_grad, grad_gate, grad_up, grad_down)
+    grad_gate, grad_up, grad_down = products(routed, grads, gate_delta, up_delta, active)
+    return (
+        residual_grad, query_grad, key_grad, value_grad, grad_gate[None], grad_up[None], grad_down[None]
+    )
 
 
 def solution(mesh):

time: 218 us -> 195 us (0.89)
  matrix products: 11.2 us -> 0 us
  other arithmetic: 10.6 us -> 0 us
  local copies, waits for them, and re-layouts: 8.83 us -> 4.81 us
  Pallas kernels: 185 us -> 188 us
    dot_general x5 -> x0, matrix products: 11.2 us -> none  [the longest x3 8.52 us: contract(): lax.dot_general(left, right, (((left_dim,), (right_dim,)), ((), ())), pre...]
    pallas_call x0 -> x1, Pallas kernels: none -> 9.42 us  [products(): pl.pallas_call(products_kernel, grid=(features // width,), out_shape=[jax...]
    pallas_call x1, Pallas kernels: 185 us -> 179 us  [fused(): pl.pallas_call(kernel, out_shape=[shape(length, features), shape(rows, fe...]
    convert_element_type x6 -> x0, other arithmetic: 4.13 us -> none  [the longest x2 2.13 us: local(): column = router_columns[:, 0].astype(jnp.float32)]
    reshape x4 -> x0, local copies, waits for them, and re-layouts: 2.62 us -> none  [the longest x2 1.33 us: wide(): jnp.broadcast_to(vector.reshape(4, 1, -1), (4, CAPL, vector.size // 4))]
where the time goes in v3:
time: 195 us; the launch traced here: 194 us
  Pallas kernels  188 us (96%)
  local copies, waits for them, and re-layouts  4.81 us (2%)
    pallas_call x1, Pallas kernels, fused(): pl.pallas_call(kernel, out_shape=[shape(length, features), shape(rows, fe...  179 us
    pallas_call x1, Pallas kernels, products(): pl.pallas_call(products_kernel, grid=(features // width,), out_shape=[jax...  9.42 us

profile of v3, /device:TPU:0, one launch (start us, length us, event | category | flops | bytes accessed | tf_op | source)
XLA Modules:
  0.0 193.7 jit_solution(15413734561169369839)
XLA Ops:
  0.6 1.3 broadcast_in_dim.20.gain
  2.0 178.8 %shard_map.180 = (bf16[256,5120]{1,0:T(8,128)(2,1)}, bf16[128,5120]{1,0:T(8,128)(2,1)}, bf16[128,5120]{1,0:T(8,128)(2,1)}, bf16[128,256]{1,0:T(8,128)(2,1)}, bf1...) custom-call(bf16[256,128]{1,0:T(8,128)(2,1)} %kin.1, ...), custom_call_target="tpu_custom_call" | custom-call | tf_op jit(solution)/shard_map/pallas_call | solution.py:673
  180.7 0.0 copy-start
  180.8 9.4 %shard_map.181 = (bf16[5120,256]{1,0:T(8,128)(2,1)}, bf16[5120,256]{1,0:T(8,128)(2,1)}, bf16[256,5120]{1,0:T(8,128)(2,1)}) custom-call(bf16[128,5120]{1,0:T(8,128)(2,1)} %get-tuple-element.23.routed, bf16[128,5120]{1,0:T(8,128)(2,1)} %get-tuple-element.24.grads, bf16[128,256]{1,0:T(8,128)(2,1)} %get-tuple-element.25.gd, ...), custom_call_target="tpu_custom_call" | custom-call | tf_op jit(solution)/shard_map/pallas_call | solution.py:770
  190.2 0.0 copy-done
  190.2 0.0 copy-start.1
  190.2 0.0 copy-start.3
  190.2 0.0 copy-start.2
  190.2 1.5 copy.24
  191.7 0.0 copy-done.1
  191.7 0.7 copy.25
  192.4 0.0 copy-done.3
  192.4 0.6 copy.26
  193.1 0.0 copy-done.2
  193.1 0.6 copy.27
Async XLA Ops:
  180.7 9.4 %copy-start = (bf16[256,5120]{1,0:T(8,128)(2,1)S(1)}, bf16[256,5120]{1,0:T(8,128)(2,1)}, u32[]{:S(2)}) copy-start(bf16[256,5120]{1,0:T(8,128)(2,1)} %get-tuple-element.38) | copy-start | bytes 7864324
  190.2 1.5 copy-start.1
  190.2 2.2 %copy-start.3 = (bf16[256,128]{1,0:T(8,128)(2,1)S(1)}, bf16[256,128]{1,0:T(8,128)(2,1)}, u32[]{:S(2)}) copy-start(bf16[256,128]{1,0:T(8,128)(2,1)} %get-tuple-element.40) | copy-start | bytes 196612
  190.2 2.9 %copy-start.2 = (bf16[256,128]{1,0:T(8,128)(2,1)S(1)}, bf16[256,128]{1,0:T(8,128)(2,1)}, u32[]{:S(2)}) copy-start(bf16[256,128]{1,0:T(8,128)(2,1)} %get-tuple-element.41) | copy-start | bytes 196612

commit v4 on v3

--- a/solution.py
+++ b/solution.py
@@ -228,8 +228,8 @@
     kin, v, wt, q, doc, eid, gain, column, gate_hbm, up_hbm, down_hbm, og_hbm, residual_hbm,
     res_out, routed_out, grads_out, gd_out, ud_out, act_out, dq, dk, dv,
     hbuf, gbuf, kbuf, vbuf, wbbuf, wabuf, gu, down, og, res, perm, perm_t, hx, grads, routed,
-    gd, ud, act, part, slots, rows, kxe, vxe, qx, gx, ot, top, sb, pb, lb, qs, gs, dqt,
-    acc, hid, grd, kx, scat, gain16, column16, pk, pv, ak, ck, bk, ek, av, cv, bv, ev,
+    gd, ud, act, pa, pb_, rows, kxe, vxe, qx, gx, ot, top, sb, pb, lb, qs, gs, dqt,
+    acc, hid, grd, kx, scat, gain16, column16, pk, pv, ak, ck, bk, ek, av, cv, bv, ev, ah, ch, bh, eh, ai, ci, bi, ei,
     gsend, grecv, glocal, send, recv, tsend, trecv, dsend, drecv, loads, stores,
 ):
     me = lax.axis_index("ctx")
@@ -251,11 +251,11 @@
     fetch_up.start()
     fetch_down.start()
 
-    def greet(d, _):
-        signal({"ctx": (me + d) % CTX})
-        return 0
-
-    lax.fori_loop(1, CTX, greet, 0)
+    y, z, x = place_of()
+    signal(at(y, z, 1 - x))
+    for d in (1, 3):
+        signal(at(y, (z + d) % NZ, x))
+        signal(at((y + d) % NY, z, x))
     for d in range(1, TP):
         signal({"tp": (tp + d) % TP})
 
@@ -282,7 +282,7 @@
             take = jnp.where((row16 >> 2) == i, mine, 0.0).astype(jnp.bfloat16)
             picked += dot(take, src[:, i * quarter : (i + 1) * quarter])
         dst[...] = picked.astype(jnp.bfloat16)
-    pl.semaphore_wait(pltpu.get_barrier_semaphore(), CTX - 1 + TP - 1)
+    pl.semaphore_wait(pltpu.get_barrier_semaphore(), 5 + TP - 1)
 
     def piece(src, buf, order, i):
         return Gather(src, buf, order, gsend.at[i], grecv.at[i], glocal.at[i])
@@ -336,6 +336,7 @@
     go(moe, 5)
     go(weights, 3)
     go(keys, 4)
+    go(weights, 4)
     go(moe, 6)
 
 
@@ -394,21 +395,22 @@
     lax.fori_loop(0, 8, back, 0)
 
     def fold(t, _):
-        cols = pl.ds(pl.multiple_of(t * 256, 256), 256)
-        part[:, :, cols] = dot(perm[...], hx[:, cols]).astype(jnp.bfloat16).reshape(CTX, 16, 256)
+        cols = pl.ds(pl.multiple_of(t * 128, 128), 128)
+        block = dot(perm[...], hx[:, cols]).astype(jnp.bfloat16)
+        pa[:, :, :, :, cols] = block.reshape(NY, NZ, NX, 16, 128)
+        cols = pl.ds(pl.multiple_of(quarter // 2 + t * 128, 128), 128)
+        block = dot(perm[...], hx[:, cols]).astype(jnp.bfloat16)
+        cols = pl.ds(pl.multiple_of(t * 128, 128), 128)
+        pb_[:, :, :, :, cols] = block.reshape(NY, NZ, NX, 16, 128)
         return 0
 
     lax.fori_loop(0, quarter // 256, fold, 0)
-
-    def partial(d):
-        to = (me + d) % CTX
-        return remote(part.at[to], slots.at[me], send.at[d], recv.at[d], {"ctx": to})
-
-    def launch(d, _):
-        partial(d).start()
-        return 0
-
-    lax.fori_loop(1, CTX, launch, 0)
+    expert_sums = [
+        Scatter(pa, ah, ch, bh, eh, 0, send.at[0], recv.at[0]),
+        Scatter(pb_, ai, ci, bi, ei, 1, send.at[1], recv.at[1]),
+    ]
+    for part_ in expert_sums:
+        part_.far(1)
     saves = [
         pltpu.make_async_copy(src, dst, stores.at[i])
         for i, (src, dst) in enumerate(
@@ -417,7 +419,8 @@
     ]
     for save in saves:
         save.start()
-    go(weights, 4)
+    for part_ in expert_sums:
+        part_.near(1)
     go(keys, 6)
 
     counts = jnp.sum(kbuf[:, :, :, length:, :].astype(jnp.float32), axis=(0, 1, 2))[:8]
@@ -479,18 +482,25 @@
         forward(me - i, False)
         return 0
 
+    def forward_part(k):
+        lax.fori_loop(1 + me * k // 5, 1 + me * (k + 1) // 5, forward_step, 0)
+
     forward(me, True)
-    half = (me + 1) // 2
-    lax.fori_loop(1, half, forward_step, 0)
+    forward_part(0)
+    for part_ in expert_sums:
+        part_.own(1)
+        part_.far(2)
+    forward_part(1)
+    for part_ in expert_sums:
+        part_.near(2)
     go(weights, 5)
-    lax.fori_loop(jnp.maximum(half, 1), me + 1, forward_step, 0)
-
-    def collect(d, sums):
-        source = (me + CTX - d) % CTX
-        remote(part.at[me], slots.at[source], send.at[d], recv.at[d], {"ctx": source}).wait_recv()
-        return sums + slots[source].astype(jnp.float32)
-
-    routed_grad = lax.fori_loop(1, CTX, collect, part[me].astype(jnp.float32))
+    forward_part(2)
+    for part_ in expert_sums:
+        part_.own(2)
+        part_.last()
+    forward_part(3)
+
+    routed_grad = jnp.concatenate([part_.total() for part_ in expert_sums], axis=1)
     hidden = hid[...].astype(jnp.float32)
     inverse = lax.rsqrt(
         fold_rows(jnp.sum(hidden * hidden, axis=1, keepdims=True)) * (1.0 / features) + EPS
@@ -511,6 +521,8 @@
 
     for d in range(1, TP):
         swap(d, tp).start()
+    forward_part(4)
+
     for d in range(1, TP):
         swap(d, (tp + TP - d) % TP).wait_recv()
 
@@ -643,11 +655,8 @@
     for part_ in sums:
         part_.finish()
 
-    def drain_partial(d, _):
-        partial(d).wait_send()
-        return 0
-
-    lax.fori_loop(1, CTX, drain_partial, 0)
+    for part_ in expert_sums:
+        part_.finish()
     for d in range(1, TP):
         swap(d, tp).wait_send()
     for piece_ in moe + keys + weights:
@@ -704,8 +713,8 @@
             pltpu.VMEM((rows, hidden), bf16),
             pltpu.VMEM((rows, hidden), bf16),
             pltpu.VMEM((rows, hidden), bf16),
-            pltpu.VMEM((CTX, 16, features // 4), bf16),
-            pltpu.VMEM((CTX, 16, features // 4), bf16),
+            pltpu.VMEM((NY, NZ, NX, 16, features // 8), bf16),
+            pltpu.VMEM((NY, NZ, NX, 16, features // 8), bf16),
             pltpu.VMEM((TP, 16, features // 4), bf16),
             pltpu.VMEM((CTX * length, 2 * HD), bf16),
             pltpu.VMEM((CTX * length, 2 * HD), bf16),
@@ -736,11 +745,19 @@
             pltpu.VMEM((2, 4, 2, length, HD), bf16),
             pltpu.VMEM((3, 1, length, HD), bf16),
             pltpu.VMEM((2, 2, length, HD), bf16),
+            pltpu.VMEM((2, 2, 2, 16, features // 8), bf16),
+            pltpu.VMEM((2, 4, 2, 16, features // 8), bf16),
+            pltpu.VMEM((3, 1, 16, features // 8), bf16),
+            pltpu.VMEM((2, 2, 16, features // 8), bf16),
+            pltpu.VMEM((2, 2, 2, 16, features // 8), bf16),
+            pltpu.VMEM((2, 4, 2, 16, features // 8), bf16),
+            pltpu.VMEM((3, 1, 16, features // 8), bf16),
+            pltpu.VMEM((2, 2, 16, features // 8), bf16),
             pltpu.SemaphoreType.DMA((6, 9)),
             pltpu.SemaphoreType.DMA((6, 9)),
             pltpu.SemaphoreType.DMA((6,)),
-            pltpu.SemaphoreType.DMA((CTX,)),
-            pltpu.SemaphoreType.DMA((CTX,)),
+            pltpu.SemaphoreType.DMA((2, 9)),
+            pltpu.SemaphoreType.DMA((2, 9)),
             pltpu.SemaphoreType.DMA((TP,)),
             pltpu.SemaphoreType.DMA((TP,)),
             pltpu.SemaphoreType.DMA((2, 9)),
@@ -752,32 +769,6 @@
             collective_id=1, has_side_effects=True, vmem_limit_bytes=60 << 20
         ),
     )(kin, v, wt, q, doc, eid, gain, column, gate, up, down, og, residual)
-
-
-def products_kernel(routed, grads, gd, ud, act, gate, up, down):
-    gate[...] = contract(routed[...], gd[...], 0, 0).astype(jnp.bfloat16)
-    up[...] = contract(routed[...], ud[...], 0, 0).astype(jnp.bfloat16)
-    down[...] = contract(act[...], grads[...], 0, 0).astype(jnp.bfloat16)
-
-
-def products(routed, grads, gd, ud, act):
-    rows, features = routed.shape
-    hidden = gd.shape[1]
-    width = 512
-    tall = pl.BlockSpec((width, hidden), lambda i: (i, 0))
-    wide = pl.BlockSpec((rows, width), lambda i: (0, i))
-    fixed = pl.BlockSpec((rows, hidden), lambda i: (0, 0))
-    return pl.pallas_call(
-        products_kernel,
-        grid=(features // width,),
-        out_shape=[
-            jax.ShapeDtypeStruct((features, hidden), jnp.bfloat16),
-            jax.ShapeDtypeStruct((features, hidden), jnp.bfloat16),
-            jax.ShapeDtypeStruct((hidden, features), jnp.bfloat16),
-        ],
-        in_specs=[wide, wide, fixed, fixed, fixed],
-        out_specs=[tall, tall, pl.BlockSpec((hidden, width), lambda i: (0, i))],
-    )(routed, grads, gd, ud, act)
 
 
 def local(
@@ -810,7 +801,9 @@
         out_grad,
         residual,
     )
-    grad_gate, grad_up, grad_down = products(routed, grads, gate_delta, up_delta, active)
+    grad_gate = contract(routed, gate_delta, 0, 0).astype(jnp.bfloat16)
+    grad_up = contract(routed, up_delta, 0, 0).astype(jnp.bfloat16)
+    grad_down = contract(active, grads, 0, 0).astype(jnp.bfloat16)
     return (
         residual_grad, query_grad, key_grad, value_grad, grad_gate[None], grad_up[None], grad_down[None]
     )

time: 195 us -> 185 us (0.949)
  Pallas kernels: 188 us -> 169 us
  matrix products: 0 us -> 8.52 us
    pallas_call x1, Pallas kernels: 179 us -> 169 us  [fused(): pl.pallas_call(kernel, out_shape=[shape(length, features), shape(rows, fe...]
    pallas_call x1 -> x0, Pallas kernels: 9.42 us -> none  [products(): pl.pallas_call(products_kernel, grid=(features // width,), out_shape=[jax...]
    dot_general x0 -> x3, matrix products: none -> 8.52 us  [contract(): lax.dot_general(left, right, (((left_dim,), (right_dim,)), ((), ())), pre...]
where the time goes in v4:
time: 185 us; the launch traced here: 183 us
  Pallas kernels  169 us (91%)
  matrix products  8.52 us (5%)
  local copies, waits for them, and re-layouts  4.83 us (3%)
    pallas_call x1, Pallas kernels, fused(): pl.pallas_call(kernel, out_shape=[shape(length, features), shape(rows, fe...  169 us
    dot_general x3, matrix products, contract(): lax.dot_general(left, right, (((left_dim,), (right_dim,)), ((), ())), pre...  8.52 us

profile of v4, /device:TPU:0, one launch (start us, length us, event | category | flops | bytes accessed | tf_op | source)
XLA Modules:
  0.0 182.8 jit_solution(6354961358742086896)
XLA Ops:
  0.6 1.3 broadcast_in_dim.20.gain
  2.0 168.8 %shard_map.180 = (bf16[256,5120]{1,0:T(8,128)(2,1)}, bf16[128,5120]{1,0:T(8,128)(2,1)}, bf16[128,5120]{1,0:T(8,128)(2,1)}, bf16[128,256]{1,0:T(8,128)(2,1)}, bf1...) custom-call(bf16[256,128]{1,0:T(8,128)(2,1)} %kin.1, ...), custom_call_target="tpu_custom_call" | custom-call | tf_op jit(solution)/shard_map/pallas_call | solution.py:682
  170.7 0.0 copy-start
  170.8 0.0 copy-start.5
  170.8 3.8 %fusion = bf16[1,5120,256]{2,1,0:T(8,128)(2,1)} fusion(bf16[128,5120]{1,0:T(8,128)(2,1)} %get-tuple-element.20, bf16[128,256]{1,0:T(8,128)(2,1)} %get-tuple-element.21), kind=kOutput, calls=%fused_computation.3 | convolution fusion | flops 336855040 | bytes 3997696 | tf_op jit(solution)/shard_map/dot_general | solution.py:20
  174.6 0.0 copy-done
  174.6 0.0 copy-done.5
  174.6 0.0 copy-start.2
  174.6 0.0 copy-start.4
  174.6 2.4 %fusion.1 = bf16[1,5120,256]{2,1,0:T(8,128)(2,1)} fusion(bf16[128,5120]{1,0:T(8,128)(2,1)S(1)} %copy-done, bf16[128,256]{1,0:T(8,128)(2,1)S(1)} %copy-done.5), kind=kOutput, calls=%fused_computation.4 | convolution fusion | flops 336855040 | bytes 3997696 | tf_op jit(solution)/shard_map/dot_general | solution.py:20
  176.9 0.0 copy-done.2
  177.0 0.0 copy-done.4
  177.0 0.0 copy-start.1
  177.0 2.4 %fusion.2 = bf16[1,256,5120]{2,1,0:T(8,128)(2,1)} fusion(bf16[128,256]{1,0:T(8,128)(2,1)S(1)} %copy-done.4, bf16[128,5120]{1,0:T(8,128)(2,1)S(1)} %copy-done.2), kind=kOutput, calls=%fused_computation.5 | convolution fusion | flops 336855040 | bytes 3997696 | tf_op jit(solution)/shard_map/dot_general | solution.py:20
  179.3 0.0 copy-done.1
  179.3 0.0 copy-start.3
  179.3 0.0 copy-start.7
  179.3 0.0 copy-start.6
  179.3 1.5 copy.24
  180.8 0.0 copy-done.3
  180.8 0.7 copy.25
  181.5 0.0 copy-done.7
  181.6 0.6 copy.26
  182.2 0.0 copy-done.6
  182.2 0.6 copy.27
Async XLA Ops:
  170.7 3.8 %copy-start = (bf16[128,5120]{1,0:T(8,128)(2,1)S(1)}, bf16[128,5120]{1,0:T(8,128)(2,1)}, u32[]{:S(2)}) copy-start(bf16[128,5120]{1,0:T(8,128)(2,1)} %get-tuple-element.20) | copy-start | bytes 3932164
  170.8 3.8 %copy-start.5 = (bf16[128,256]{1,0:T(8,128)(2,1)S(1)}, bf16[128,256]{1,0:T(8,128)(2,1)}, u32[]{:S(2)}) copy-start(bf16[128,256]{1,0:T(8,128)(2,1)} %get-tuple-element.22) | copy-start | bytes 196612
  174.6 2.4 %copy-start.2 = (bf16[128,5120]{1,0:T(8,128)(2,1)S(1)}, bf16[128,5120]{1,0:T(8,128)(2,1)}, u32[]{:S(2)}) copy-start(bf16[128,5120]{1,0:T(8,128)(2,1)} %get-tuple-element.24) | copy-start | bytes 3932164
  174.6 2.4 %copy-start.4 = (bf16[128,256]{1,0:T(8,128)(2,1)S(1)}, bf16[128,256]{1,0:T(8,128)(2,1)}, u32[]{:S(2)}) copy-start(bf16[128,256]{1,0:T(8,128)(2,1)} %get-tuple-element.23) | copy-start | bytes 196612
  177.0 2.4 %copy-start.1 = (bf16[256,5120]{1,0:T(8,128)(2,1)S(1)}, bf16[256,5120]{1,0:T(8,128)(2,1)}, u32[]{:S(2)}) copy-start(bf16[256,5120]{1,0:T(8,128)(2,1)} %get-tuple-element.32) | copy-start | bytes 7864324
  179.3 1.5 copy-start.3
  179.3 2.2 %copy-start.7 = (bf16[256,128]{1,0:T(8,128)(2,1)S(1)}, bf16[256,128]{1,0:T(8,128)(2,1)}, u32[]{:S(2)}) copy-start(bf16[256,128]{1,0:T(8,128)(2,1)} %get-tuple-element.34) | copy-start | bytes 196612
  179.3 2.9 %copy-start.6 = (bf16[256,128]{1,0:T(8,128)(2,1)S(1)}, bf16[256,128]{1,0:T(8,128)(2,1)}, u32[]{:S(2)}) copy-start(bf16[256,128]{1,0:T(8,128)(2,1)} %get-tuple-element.35) | copy-start | bytes 196612

commit v5 on v4

--- a/solution.py
+++ b/solution.py
@@ -200,6 +200,39 @@
         self.swap().wait_send()
 
 
+class Share(Scatter):
+    def pair(self, d):
+        y, z, x = place_of()
+        inner = (z if self.order == 0 else y) * 2 + x
+        to, source = (inner + d) % 8, (inner + 8 - d) % 8
+        if self.order == 0:
+            src, there = self.p.at[y, to // 2, to % 2], at(y, to // 2, to % 2)
+        else:
+            src, there = self.p.at[to // 2, z, to % 2], at(to // 2, z, to % 2)
+        return remote(
+            src, self.far_in[1].at[d], self.send.at[4 + d], self.recv.at[4 + d], there
+        )
+
+    def spread(self):
+        for d in range(1, 8):
+            self.pair(d).start()
+
+    def total(self):
+        y, z, x = place_of()
+        total = self.p[y, z, x].astype(jnp.float32)
+        for d in range(1, 8):
+            self.pair(d).wait_recv()
+            total += self.far_in[1][d].astype(jnp.float32)
+        return total
+
+    def finish(self):
+        for near in (0, 1):
+            for copy in self.copies(1, near):
+                copy.wait_send()
+        for d in range(1, 8):
+            self.pair(d).wait_send()
+
+
 BIG = 2.0**60
 
 
@@ -229,7 +262,7 @@
     res_out, routed_out, grads_out, gd_out, ud_out, act_out, dq, dk, dv,
     hbuf, gbuf, kbuf, vbuf, wbbuf, wabuf, gu, down, og, res, perm, perm_t, hx, grads, routed,
     gd, ud, act, pa, pb_, rows, kxe, vxe, qx, gx, ot, top, sb, pb, lb, qs, gs, dqt,
-    acc, hid, grd, kx, scat, gain16, column16, pk, pv, ak, ck, bk, ek, av, cv, bv, ev, ah, ch, bh, eh, ai, ci, bi, ei,
+    acc, hid, grd, kx, scat, gain16, column16, pk, pv, ak, ck, bk, av, cv, bv, ah, ch, bh, eh, ai, ci, bi, ei,
     gsend, grecv, glocal, send, recv, tsend, trecv, dsend, drecv, loads, stores,
 ):
     me = lax.axis_index("ctx")
@@ -252,10 +285,12 @@
     fetch_down.start()
 
     y, z, x = place_of()
-    signal(at(y, z, 1 - x))
-    for d in (1, 3):
-        signal(at(y, (z + d) % NZ, x))
-        signal(at((y + d) % NY, z, x))
+    for d in range(1, 8):
+        to = (z * 2 + x + d) % 8
+        signal(at(y, to // 2, to % 2))
+    for d in range(1, 4):
+        for e in (0, 1):
+            signal(at((y + d) % NY, z, (x + e) % 2))
     for d in range(1, TP):
         signal({"tp": (tp + d) % TP})
 
@@ -282,7 +317,7 @@
             take = jnp.where((row16 >> 2) == i, mine, 0.0).astype(jnp.bfloat16)
             picked += dot(take, src[:, i * quarter : (i + 1) * quarter])
         dst[...] = picked.astype(jnp.bfloat16)
-    pl.semaphore_wait(pltpu.get_barrier_semaphore(), 5 + TP - 1)
+    pl.semaphore_wait(pltpu.get_barrier_semaphore(), 13 + TP - 1)
 
     def piece(src, buf, order, i):
         return Gather(src, buf, order, gsend.at[i], grecv.at[i], glocal.at[i])
@@ -591,8 +626,8 @@
         pv[y, z, x] = value_sum.astype(jnp.bfloat16)
 
     sums = [
-        Scatter(pk, ak, ck, bk, ek, 0, dsend.at[0], drecv.at[0]),
-        Scatter(pv, av, cv, bv, ev, 1, dsend.at[1], drecv.at[1]),
+        Share(pk, ak, ck, bk, None, 0, dsend.at[0], drecv.at[0]),
+        Share(pv, av, cv, bv, None, 1, dsend.at[1], drecv.at[1]),
     ]
     y, z, x = place_of()
     for h in range(heads):
@@ -642,14 +677,9 @@
     lax.fori_loop(0, CTX, backward_step, 0)
     for part_ in sums:
         part_.own(1)
-        part_.far(2)
+        part_.spread()
     for h in range(heads):
         dq[:, h * HD : (h + 1) * HD] = (dqt[h].T * scale).astype(jnp.bfloat16)
-    for part_ in sums:
-        part_.near(2)
-    for part_ in sums:
-        part_.own(2)
-        part_.last()
     dk[...] = sums[0].total().astype(jnp.bfloat16)
     dv[...] = sums[1].total().astype(jnp.bfloat16)
     for part_ in sums:
@@ -739,12 +769,10 @@
             pltpu.VMEM((NY, NZ, NX, length, HD), bf16),
             pltpu.VMEM((2, 2, 2, length, HD), bf16),
             pltpu.VMEM((2, 4, 2, length, HD), bf16),
-            pltpu.VMEM((3, 1, length, HD), bf16),
-            pltpu.VMEM((2, 2, length, HD), bf16),
+            pltpu.VMEM((8, length, HD), bf16),
             pltpu.VMEM((2, 2, 2, length, HD), bf16),
             pltpu.VMEM((2, 4, 2, length, HD), bf16),
-            pltpu.VMEM((3, 1, length, HD), bf16),
-            pltpu.VMEM((2, 2, length, HD), bf16),
+            pltpu.VMEM((8, length, HD), bf16),
             pltpu.VMEM((2, 2, 2, 16, features // 8), bf16),
             pltpu.VMEM((2, 4, 2, 16, features // 8), bf16),
             pltpu.VMEM((3, 1, 16, features // 8), bf16),
@@ -760,8 +788,8 @@
             pltpu.SemaphoreType.DMA((2, 9)),
             pltpu.SemaphoreType.DMA((TP,)),
             pltpu.SemaphoreType.DMA((TP,)),
-            pltpu.SemaphoreType.DMA((2, 9)),
-            pltpu.SemaphoreType.DMA((2, 9)),
+            pltpu.SemaphoreType.DMA((2, 12)),
+            pltpu.SemaphoreType.DMA((2, 12)),
             pltpu.SemaphoreType.DMA((5,)),
             pltpu.SemaphoreType.DMA((6,)),
         ],

time: 185 us -> 185 us (level)
  no operation moved by 1% of the time
where the time goes in v5:
time: 185 us; the launch traced here: 183 us
  Pallas kernels  169 us (91%)
  matrix products  8.52 us (5%)
  local copies, waits for them, and re-layouts  4.83 us (3%)
    pallas_call x1, Pallas kernels, fused(): pl.pallas_call(kernel, out_shape=[shape(length, features), shape(rows, fe...  169 us
    dot_general x3, matrix products, contract(): lax.dot_general(left, right, (((left_dim,), (right_dim,)), ((), ())), pre...  8.52 us

profile of v5, /device:TPU:0, one launch (start us, length us, event | category | flops | bytes accessed | tf_op | source)
XLA Modules:
  0.0 183.0 jit_solution(16448408464496221374)
XLA Ops:
  0.6 1.3 broadcast_in_dim.20.gain
  2.0 169.0 %shard_map.180 = (bf16[256,5120]{1,0:T(8,128)(2,1)}, bf16[128,5120]{1,0:T(8,128)(2,1)}, bf16[128,5120]{1,0:T(8,128)(2,1)}, bf16[128,256]{1,0:T(8,128)(2,1)}, bf1...) custom-call(bf16[256,128]{1,0:T(8,128)(2,1)} %kin.1, ...), custom_call_target="tpu_custom_call" | custom-call | tf_op jit(solution)/shard_map/pallas_call | solution.py:712
  170.9 0.0 copy-start
  171.0 0.0 copy-start.5
  171.0 3.8 %fusion = bf16[1,5120,256]{2,1,0:T(8,128)(2,1)} fusion(bf16[128,5120]{1,0:T(8,128)(2,1)} %get-tuple-element.20, bf16[128,256]{1,0:T(8,128)(2,1)} %get-tuple-element.21), kind=kOutput, calls=%fused_computation.3 | convolution fusion | flops 336855040 | bytes 3997696 | tf_op jit(solution)/shard_map/dot_general | solution.py:20
  174.8 0.0 copy-done
  174.8 0.0 copy-done.5
  174.8 0.0 copy-start.2
  174.8 0.0 copy-start.4
  174.8 2.4 %fusion.1 = bf16[1,5120,256]{2,1,0:T(8,128)(2,1)} fusion(bf16[128,5120]{1,0:T(8,128)(2,1)S(1)} %copy-done, bf16[128,256]{1,0:T(8,128)(2,1)S(1)} %copy-done.5), kind=kOutput, calls=%fused_computation.4 | convolution fusion | flops 336855040 | bytes 3997696 | tf_op jit(solution)/shard_map/dot_general | solution.py:20
  177.1 0.0 copy-done.2
  177.2 0.0 copy-done.4
  177.2 0.0 copy-start.1
  177.2 2.4 %fusion.2 = bf16[1,256,5120]{2,1,0:T(8,128)(2,1)} fusion(bf16[128,256]{1,0:T(8,128)(2,1)S(1)} %copy-done.4, bf16[128,5120]{1,0:T(8,128)(2,1)S(1)} %copy-done.2), kind=kOutput, calls=%fused_computation.5 | convolution fusion | flops 336855040 | bytes 3997696 | tf_op jit(solution)/shard_map/dot_general | solution.py:20
  179.5 0.0 copy-done.1
  179.5 0.0 copy-start.3
  179.5 0.0 copy-start.7
  179.5 0.0 copy-start.6
  179.5 1.5 copy.24
  181.0 0.0 copy-done.3
  181.0 0.7 copy.25
  181.8 0.0 copy-done.7
  181.8 0.6 copy.26
  182.4 0.0 copy-done.6
  182.4 0.6 copy.27
Async XLA Ops:
  170.9 3.8 %copy-start = (bf16[128,5120]{1,0:T(8,128)(2,1)S(1)}, bf16[128,5120]{1,0:T(8,128)(2,1)}, u32[]{:S(2)}) copy-start(bf16[128,5120]{1,0:T(8,128)(2,1)} %get-tuple-element.20) | copy-start | bytes 3932164
  171.0 3.8 %copy-start.5 = (bf16[128,256]{1,0:T(8,128)(2,1)S(1)}, bf16[128,256]{1,0:T(8,128)(2,1)}, u32[]{:S(2)}) copy-start(bf16[128,256]{1,0:T(8,128)(2,1)} %get-tuple-element.22) | copy-start | bytes 196612
  174.8 2.4 %copy-start.2 = (bf16[128,5120]{1,0:T(8,128)(2,1)S(1)}, bf16[128,5120]{1,0:T(8,128)(2,1)}, u32[]{:S(2)}) copy-start(bf16[128,5120]{1,0:T(8,128)(2,1)} %get-tuple-element.24) | copy-start | bytes 3932164
  174.8 2.4 %copy-start.4 = (bf16[128,256]{1,0:T(8,128)(2,1)S(1)}, bf16[128,256]{1,0:T(8,128)(2,1)}, u32[]{:S(2)}) copy-start(bf16[128,256]{1,0:T(8,128)(2,1)} %get-tuple-element.23) | copy-start | bytes 196612
  177.2 2.4 %copy-start.1 = (bf16[256,5120]{1,0:T(8,128)(2,1)S(1)}, bf16[256,5120]{1,0:T(8,128)(2,1)}, u32[]{:S(2)}) copy-start(bf16[256,5120]{1,0:T(8,128)(2,1)} %get-tuple-element.32) | copy-start | bytes 7864324
  179.5 1.5 copy-start.3
  179.5 2.2 %copy-start.7 = (bf16[256,128]{1,0:T(8,128)(2,1)S(1)}, bf16[256,128]{1,0:T(8,128)(2,1)}, u32[]{:S(2)}) copy-start(bf16[256,128]{1,0:T(8,128)(2,1)} %get-tuple-element.34) | copy-start | bytes 196612
  179.5 2.9 %copy-start.6 = (bf16[256,128]{1,0:T(8,128)(2,1)S(1)}, bf16[256,128]{1,0:T(8,128)(2,1)}, u32[]{:S(2)}) copy-start(bf16[256,128]{1,0:T(8,128)(2,1)} %get-tuple-element.35) | copy-start | bytes 196612
